TPU v7x, 32 devices: a whole 2x2x4 slice. The times are simulated.
32 devices in a mesh: blk: 32 (over z, y, x, core).
Axes of the slice: x: 2, y: 2, z: 4, core: 2. Of those that a mesh axis runs over, the one named last changes fastest.
Arguments:
- text_tokens: bfloat16 [8192, 768], P('blk'), may hold values from -6 to 6
- segment_ids: int32 [128, 64], P('blk'), may hold values from 0 to 3, never falling along the last dimension, each value on 1 to 28 neighbouring positions
- pair_index: int32 [512], P('blk'), may hold values from 0 to 511, each once
- image_tokens: bfloat16 [25600, 768], P('blk'), may hold values from -6 to 6
- logit_scale: float32 [1], replicated, may hold values from 30 to 90
- img_gains: bfloat16 [1536], P('blk'), may hold values from 0.5 to 1.5
- img_shifts: bfloat16 [1536], P('blk'), may hold values from -2 to 2
- img_qkv: bfloat16 [768, 2304], P('blk'), may hold values from -0.21875 to 0.21875
- img_out: bfloat16 [768, 768], P('blk'), may hold values from -1.25 to 1.25
- img_in: bfloat16 [768, 3072], P('blk'), may hold values from -0.21875 to 0.21875
- img_down: bfloat16 [3072, 768], P('blk'), may hold values from -0.15625 to 0.15625
- img_biases: bfloat16 [3840], P('blk'), may hold values from -2 to 2
- img_proj: bfloat16 [768, 768], P('blk'), may hold values from -0.21875 to 0.21875
- txt_gains: bfloat16 [1536], P('blk'), may hold values from 0.5 to 1.5
- txt_shifts: bfloat16 [1536], P('blk'), may hold values from -2 to 2
- txt_qkv: bfloat16 [768, 2304], P('blk'), may hold values from -0.21875 to 0.21875
- txt_out: bfloat16 [768, 768], P('blk'), may hold values from -0.875 to 0.875
- txt_in: bfloat16 [768, 3072], P('blk'), may hold values from -0.21875 to 0.21875
- txt_down: bfloat16 [3072, 768], P('blk'), may hold values from -0.15625 to 0.15625
- txt_biases: bfloat16 [3840], P('blk'), may hold values from -2 to 2
- txt_proj: bfloat16 [768, 768], P('blk'), may hold values from -0.21875 to 0.21875
Outputs:
- pair_loss: float32 [512], P('blk')
- text_out: bfloat16 [8192, 768], P('blk')
- text_grad: float32 [8192, 768], P('blk')
- grad_gains: float32 [1536], P('blk')
- grad_shifts: float32 [1536], P('blk')
- grad_qkv: float32 [768, 2304], P('blk')
- grad_out: float32 [768, 768], P('blk')
- grad_in: float32 [768, 3072], P('blk')
- grad_down: float32 [3072, 768], P('blk')
- grad_biases: float32 [3840], P('blk')
- grad_proj: float32 [768, 768], P('blk')
Inputs may be any that keep to these rules, and one draw needn't show every extreme that they name: `segment_ids`: each row holds 4 captions in order, ids never falling, each caption 1 to 28 tokens. `pair_index`: each image belongs to exactly one caption.
All inputs are finite; a program needn't handle non-finite values.
Results may differ from a plain program's by a relative error of at most 0.018.
The roundings to bfloat16 on the way count: a program that leaves them out, or rounds other values in their place, can miss the bound.
Values may be sent and summed in bfloat16 or wider, within the bound.
No kernel may reach another device: no remote copies, remote signals or barrier semaphores. Data moves between devices by JAX's collectives and lax.ppermute only.
A program may use at most 192 MiB of HBM per device.

v0:
```python
import jax
import jax.numpy as jnp
from jax import lax
from jax.sharding import PartitionSpec as P

HEAD = 64
PATCHES = 50
CAPS = 4


HIGH = lax.Precision.HIGHEST


def gelu(z):
    return 0.5 * z * (1.0 + jnp.tanh(0.7978845608028654 * (z + 0.044715 * z * z * z)))


def normalize(x):
    mean = jnp.mean(x, axis=-1, keepdims=True)
    cent = x - mean
    rstd = lax.rsqrt(jnp.mean(cent * cent, axis=-1, keepdims=True) + 1e-06)
    return (cent * rstd, rstd)


def norm_back(grad, normed, rstd):
    return rstd * (
        grad
        - jnp.mean(grad, axis=-1, keepdims=True)
        - normed * jnp.mean(grad * normed, axis=-1, keepdims=True)
    )


def matmul(left, right):
    return jnp.dot(left, right, preferred_element_type=jnp.float32)


def left_product(left, right):
    return lax.dot_general(
        left, right, (((0,), (0,)), ((), ())), preferred_element_type=jnp.float32
    )


def right_product(left, right):
    return lax.dot_general(
        left, right, (((1,), (1,)), ((), ())), preferred_element_type=jnp.float32
    )


def attention(qkv, same):
    groups, length, triple = qkv.shape
    width = triple // 3
    heads = width // HEAD
    query = qkv[..., :width].reshape(groups, length, heads, HEAD)
    keys = qkv[..., width : 2 * width].reshape(groups, length, heads, HEAD)
    values = qkv[..., 2 * width :].reshape(groups, length, heads, HEAD)
    scores = jnp.einsum("gthd,gshd->ghts", query, keys, preferred_element_type=jnp.float32) * 0.125
    scores = jnp.where(same[:, None], scores, -1000000000.0)
    top = jnp.max(scores, axis=-1, keepdims=True)
    expo = jnp.exp(scores - top)
    probs = expo / jnp.sum(expo, axis=-1, keepdims=True)
    mixed = jnp.einsum(
        "ghts,gshd->gthd", probs.astype(jnp.bfloat16), values, preferred_element_type=jnp.float32
    )
    return (mixed.reshape(groups * length, width).astype(jnp.bfloat16), probs, query, keys, values)


def forward_block(x, same, groups, gains, shifts, w_qkv, w_out, w_in, w_down, biases):
    width = x.shape[1]
    units = w_in.shape[1]
    normed1, rstd1 = normalize(x)
    act1 = (normed1 * gains[:width] + shifts[:width]).astype(jnp.bfloat16)
    qkv = matmul(act1, w_qkv).astype(jnp.bfloat16).reshape(groups, -1, 3 * width)
    mixed, probs, query, keys, values = attention(qkv, same)
    second = x + matmul(mixed, w_out)
    normed2, rstd2 = normalize(second)
    act2 = (normed2 * gains[width:] + shifts[width:]).astype(jnp.bfloat16)
    inner = matmul(act2, w_in) + biases[:units]
    hidden = gelu(inner).astype(jnp.bfloat16)
    y = second + matmul(hidden, w_down) + biases[units:]
    return (
        y,
        (
            normed1,
            rstd1,
            act1,
            probs,
            query,
            keys,
            values,
            mixed,
            normed2,
            rstd2,
            act2,
            inner,
            hidden,
        ),
    )


def unit_rows(proj):
    factor = lax.rsqrt(jnp.sum(proj * proj, axis=-1, keepdims=True) + 1e-06)
    return (proj * factor, factor)


def on_device(
    text_tokens,
    segment_ids,
    pair_index,
    image_tokens,
    logit_scale,
    img_gains,
    img_shifts,
    img_qkv,
    img_out,
    img_in,
    img_down,
    img_biases,
    img_proj,
    txt_gains,
    txt_shifts,
    txt_qkv,
    txt_out,
    txt_in,
    txt_down,
    txt_biases,
    txt_proj,
):
    whole = (
        lax.all_gather(img_gains, "blk", axis=0, tiled=True),
        lax.all_gather(img_shifts, "blk", axis=0, tiled=True),
        lax.all_gather(img_qkv, "blk", axis=0, tiled=True),
        lax.all_gather(img_out, "blk", axis=0, tiled=True),
        lax.all_gather(img_in, "blk", axis=0, tiled=True),
        lax.all_gather(img_down, "blk", axis=0, tiled=True),
        lax.all_gather(img_biases, "blk", axis=0, tiled=True),
        lax.all_gather(img_proj, "blk", axis=0, tiled=True),
        lax.all_gather(txt_gains, "blk", axis=0, tiled=True),
        lax.all_gather(txt_shifts, "blk", axis=0, tiled=True),
        lax.all_gather(txt_qkv, "blk", axis=0, tiled=True),
        lax.all_gather(txt_out, "blk", axis=0, tiled=True),
        lax.all_gather(txt_in, "blk", axis=0, tiled=True),
        lax.all_gather(txt_down, "blk", axis=0, tiled=True),
        lax.all_gather(txt_biases, "blk", axis=0, tiled=True),
        lax.all_gather(txt_proj, "blk", axis=0, tiled=True),
    )
    image_weights = whole[:8]
    text_weights = whole[8:]
    gains, shifts, w_qkv, w_out, w_in, w_down, biases, w_proj = text_weights
    width = text_tokens.shape[1]
    scale = logit_scale[0]
    images = image_tokens.shape[0] // PATCHES
    every = jnp.ones((images, PATCHES, PATCHES), jnp.bool_)
    image_y, unused = forward_block(
        image_tokens.astype(jnp.float32), every, images, *image_weights[:7]
    )
    image_pool = jnp.mean(image_y.reshape(images, PATCHES, width), axis=1)
    image_unit, unused_factor = unit_rows(matmul(image_pool.astype(jnp.bfloat16), image_weights[7]))
    image_emb = image_unit.astype(jnp.bfloat16)
    rows, length = segment_ids.shape
    tokens = rows * length
    captions = pair_index.shape[0]
    same = segment_ids[:, :, None] == segment_ids[:, None, :]
    x = text_tokens.astype(jnp.float32)
    y, kept = forward_block(x, same, rows, gains, shifts, w_qkv, w_out, w_in, w_down, biases)
    normed1, rstd1, act1, probs, query, keys, values, mixed, normed2, rstd2, act2, inner, hidden = (
        kept
    )
    text_out = y.astype(jnp.bfloat16)
    caption_of = (jnp.arange(rows, dtype=jnp.int32)[:, None] * CAPS + segment_ids).reshape(tokens)
    member = (jnp.arange(captions, dtype=jnp.int32)[:, None] == caption_of[None, :]).astype(
        jnp.float32
    )
    member = member / jnp.sum(member, axis=1, keepdims=True)
    caption_pool = jnp.dot(member, y, precision=HIGH, preferred_element_type=jnp.float32)
    pool_low = caption_pool.astype(jnp.bfloat16)
    proj = matmul(pool_low, w_proj)
    caption_unit, factor = unit_rows(proj)
    caption_emb = caption_unit.astype(jnp.bfloat16)
    start_max = jnp.full((images,), -1e30, jnp.float32)
    col_max = start_max
    sim = scale * right_product(image_emb, lax.all_gather(caption_emb, "blk", axis=0, tiled=True))
    new_max = jnp.maximum(col_max, jnp.max(sim, axis=1))
    col_sum = jnp.sum(jnp.exp(sim - new_max[:, None]), axis=1)
    col_max, col_sum = (new_max, col_sum)
    col_lse = lax.all_gather(col_max + jnp.log(col_sum), "blk", axis=0, tiled=True)
    piece = lax.all_gather(image_emb, "blk", axis=0, tiled=True)
    row_max = jnp.full((captions,), -1e30, jnp.float32)
    sim = scale * right_product(caption_emb, piece)
    hit = pair_index[:, None] == jnp.arange(piece.shape[0], dtype=jnp.int32)[None, :]
    new_max = jnp.maximum(row_max, jnp.max(sim, axis=1))
    row_sum = jnp.sum(jnp.exp(sim - new_max[:, None]), axis=1)
    row_max, row_sum, pos = (new_max, row_sum, jnp.sum(jnp.where(hit, sim, 0.0), axis=1))
    row_lse = row_max + jnp.log(row_sum)
    pair_col = jnp.take(col_lse, pair_index)
    pair_loss = 0.5 * (row_lse - pos) + 0.5 * (pair_col - pos)
    piece = lax.all_gather(image_emb, "blk", axis=0, tiled=True)
    count = piece.shape[0]
    sim = scale * right_product(caption_emb, piece)
    hit = pair_index[:, None] == jnp.arange(count, dtype=jnp.int32)[None, :]
    weights_sim = (
        0.5 * jnp.exp(sim - row_lse[:, None])
        + 0.5 * jnp.exp(sim - col_lse[None, :])
        - hit.astype(jnp.float32)
    )
    d_emb = scale * matmul(weights_sim.astype(jnp.bfloat16), piece)
    d_proj = factor * d_emb - proj * (factor * factor * factor) * jnp.sum(
        d_emb * proj, axis=-1, keepdims=True
    )
    d_proj_low = d_proj.astype(jnp.bfloat16)
    grad_proj = left_product(pool_low, d_proj_low)
    d_pool = right_product(d_proj_low, w_proj)
    d_y = lax.dot_general(
        member, d_pool, (((0,), (0,)), ((), ())), precision=HIGH, preferred_element_type=jnp.float32
    )
    grad_outer = jnp.sum(d_y, axis=0)
    d_y_low = d_y.astype(jnp.bfloat16)
    grad_down = left_product(hidden, d_y_low)
    d_hidden = right_product(d_y_low, w_down)
    unused_value, gelu_pull = jax.vjp(gelu, inner)
    d_inner = gelu_pull(d_hidden)[0].astype(jnp.bfloat16)
    grad_in = left_product(act2, d_inner)
    grad_inner = jnp.sum(d_inner.astype(jnp.float32), axis=0)
    grad_biases = jnp.concatenate([grad_inner, grad_outer])
    d_act2 = right_product(d_inner, w_in)
    gain2 = jnp.sum(d_act2 * normed2, axis=0)
    shift2 = jnp.sum(d_act2, axis=0)
    d_second = d_y + norm_back(d_act2 * gains[width:], normed2, rstd2)
    d_second_low = d_second.astype(jnp.bfloat16)
    grad_out = left_product(mixed, d_second_low)
    d_mixed = (
        right_product(d_second_low, w_out)
        .astype(jnp.bfloat16)
        .reshape(rows, length, width // HEAD, HEAD)
    )
    probs_low = probs.astype(jnp.bfloat16)
    d_values = jnp.einsum("ghts,gthd->gshd", probs_low, d_mixed, preferred_element_type=jnp.float32)
    d_probs = jnp.einsum("gthd,gshd->ghts", d_mixed, values, preferred_element_type=jnp.float32)
    d_scores = (probs * (d_probs - jnp.sum(probs * d_probs, axis=-1, keepdims=True))).astype(
        jnp.bfloat16
    )
    d_query = 0.125 * jnp.einsum(
        "ghts,gshd->gthd", d_scores, keys, preferred_element_type=jnp.float32
    )
    d_keys = 0.125 * jnp.einsum(
        "ghts,gthd->gshd", d_scores, query, preferred_element_type=jnp.float32
    )
    d_qkv = jnp.concatenate(
        [
            d_query.reshape(tokens, width),
            d_keys.reshape(tokens, width),
            d_values.reshape(tokens, width),
        ],
        axis=1,
    ).astype(jnp.bfloat16)
    grad_qkv = left_product(act1, d_qkv)
    d_act1 = right_product(d_qkv, w_qkv)
    gain1 = jnp.sum(d_act1 * normed1, axis=0)
    shift1 = jnp.sum(d_act1, axis=0)
    text_grad = d_second + norm_back(d_act1 * gains[:width], normed1, rstd1)
    grad_gains = jnp.concatenate([gain1, gain2])
    grad_shifts = jnp.concatenate([shift1, shift2])
    summed = (
        lax.psum_scatter(grad_gains, "blk", scatter_dimension=0, tiled=True),
        lax.psum_scatter(grad_shifts, "blk", scatter_dimension=0, tiled=True),
        lax.psum_scatter(grad_qkv, "blk", scatter_dimension=0, tiled=True),
        lax.psum_scatter(grad_out, "blk", scatter_dimension=0, tiled=True),
        lax.psum_scatter(grad_in, "blk", scatter_dimension=0, tiled=True),
        lax.psum_scatter(grad_down, "blk", scatter_dimension=0, tiled=True),
        lax.psum_scatter(grad_biases, "blk", scatter_dimension=0, tiled=True),
        lax.psum_scatter(grad_proj, "blk", scatter_dimension=0, tiled=True),
    )
    return (
        pair_loss,
        text_out,
        text_grad,
        summed[0],
        summed[1],
        summed[2],
        summed[3],
        summed[4],
        summed[5],
        summed[6],
        summed[7],
    )


def solution(mesh):
    placed = (
        P("blk", None),
        P("blk", None),
        P("blk"),
        P("blk", None),
        P(),
        P("blk"),
        P("blk"),
        P("blk", None),
        P("blk", None),
        P("blk", None),
        P("blk", None),
        P("blk"),
        P("blk", None),
        P("blk"),
        P("blk"),
        P("blk", None),
        P("blk", None),
        P("blk", None),
        P("blk", None),
        P("blk"),
        P("blk", None),
    )
    return jax.shard_map(
        on_device,
        mesh=mesh,
        in_specs=placed,
        out_specs=(
            P("blk"),
            P("blk", None),
            P("blk", None),
            P("blk"),
            P("blk"),
            P("blk", None),
            P("blk", None),
            P("blk", None),
            P("blk", None),
            P("blk"),
            P("blk", None),
        ),
        check_vma=False,
    )
```

profile of v0, /device:TPU:0, one launch (start us, length us, event | category | flops | bytes accessed | tf_op | source)
XLA Modules:
  0.0 1364.6 jit_solution(6057025329942622917)
XLA Ops:
  19.1 42.8 %all-reduce.11 = (bf16[1536]{0:T(1024)(128)(2,1)S(1)}, bf16[1536]{0:T(1024)(128)(2,1)S(1)}, bf16[3840]{0:T(1024)(128)(2,1)S(1)}, bf16[1536]{0:T(1024)(128)(2,1)S...) all-reduce(bf16[1536]{0:T(1024)(128)(2,1)S(1)} %dynamic-update-slic, ...), channel_id=1, replica_groups=mesh['blk'=32] {'blk'}, use_global_device_ids=true, to_apply=%add.1 | all-reduce | flops 13824 | bytes 55296
  70.3 3.9 all-gather.21.cloned.1.call-done
  74.2 6.9 convolution_convert_fusion
  81.1 5.0 reshape.201
  86.1 4.2 fusion.99
  90.3 3.5 reshape.234
  93.8 4.8 reshape.235
  98.7 3.5 fusion.19
  102.2 4.0 fusion.104
  106.1 3.3 reshape.233
  109.4 5.2 convert_bitcast_fusion
  115.2 3.2 convert_element_type.165
  118.4 11.6 all-gather.23.cloned.1.call-done
  130.0 3.3 fusion.105
  135.7 56.2 %all-gather.11.cloned.1.call-done = bf16[768,2304]{1,0:T(8,128)(2,1)} async-done(((bf16[24,2304]{1,0:T(8,128)(2,1)}), bf16[768,2304]{1,0:T(8,128)(2,1)}) %all-gather.11.cloned.1.call-update) | async-done | bytes 3538960 | tf_op jit(solution)/shard_map/all_gather | solution.py:139
  191.9 3.2 convolution_convert_fusion.1
  206.9 40.6 %all-gather.13.cloned.1.call-done = bf16[768,768]{1,0:T(8,128)(2,1)} async-done(((bf16[24,768]{1,0:T(8,128)(2,1)}), bf16[768,768]{1,0:T(8,128)(2,1)}) %all-gather.13.cloned.1.call-update) | async-done | bytes 1179664 | tf_op jit(solution)/shard_map/all_gather | solution.py:140
  249.6 63.2 %all-gather.25.cloned.1.call-done = bf16[768,3072]{1,0:T(8,128)(2,1)} async-done(((bf16[24,3072]{1,0:T(8,128)(2,1)}), bf16[768,3072]{1,0:T(8,128)(2,1)}) %all-gather.25.cloned.1.call-update) | async-done | bytes 4718608 | tf_op jit(solution)/shard_map/all_gather | solution.py:133
  312.9 65.2 %all-gather.27.cloned.1.call-done = bf16[3072,768]{1,0:T(8,128)(2,1)} async-done(((bf16[96,768]{1,0:T(8,128)(2,1)}), bf16[3072,768]{1,0:T(8,128)(2,1)}) %all-gather.27.cloned.1.call-update) | async-done | bytes 4718608 | tf_op jit(solution)/shard_map/all_gather | solution.py:134
  378.1 15.1 %add_add_fusion = f32[800,768]{1,0:T(8,128)} fusion(f32[800,768]{1,0:T(8,128)} %copy-done.10, bf16[3072,768]{1,0:T(8,128)(2,1)} %all-gather.27.cloned.1.call-done, bf16[768,3072]{1,0:T(8,128)(2,1)} %all-gather.25.cloned.1.call-done, f32[3072]{0:T(1024)S(1)} %copy-done.29, f32[768]{0:T(1024)S(1)} %copy-done.36, f32[768]{0:T(1024)S(1)} %copy-done.40, ...), kind=kOutput, calls=%fused_computation.45 | convolution fusion | flops 7578624000 | bytes 14380288 | tf_op jit(solution)/shard_map/dot_general | solution.py:34
  393.3 3.0 reshape.205
  398.3 35.6 %all-gather.29.cloned.1.call-done = bf16[768,768]{1,0:T(8,128)(2,1)} async-done(((bf16[24,768]{1,0:T(8,128)(2,1)}), bf16[768,768]{1,0:T(8,128)(2,1)}) %all-gather.29.cloned.1.call-update) | async-done | bytes 1179664 | tf_op jit(solution)/shard_map/all_gather | solution.py:136
  435.6 63.8 %all-gather.15.cloned.1.call-done = bf16[768,3072]{1,0:T(8,128)(2,1)} async-done(((bf16[24,3072]{1,0:T(8,128)(2,1)}), bf16[768,3072]{1,0:T(8,128)(2,1)}) %all-gather.15.cloned.1.call-update) | async-done | bytes 4718608 | tf_op jit(solution)/shard_map/all_gather | solution.py:141
  499.4 5.5 convolution_add_fusion
  504.9 59.9 %all-gather.17.cloned.1.call-done = bf16[3072,768]{1,0:T(8,128)(2,1)} async-done(((bf16[96,768]{1,0:T(8,128)(2,1)}), bf16[3072,768]{1,0:T(8,128)(2,1)}) %all-gather.17.cloned.1.call-update) | async-done | bytes 4718608 | tf_op jit(solution)/shard_map/all_gather | solution.py:142
  564.8 6.0 fusion.108
  571.3 49.1 %all-gather.19.cloned.1.call-done = bf16[768,768]{1,0:T(8,128)(2,1)} async-done(((bf16[24,768]{1,0:T(8,128)(2,1)}), bf16[768,768]{1,0:T(8,128)(2,1)}) %all-gather.19.cloned.1.call-update) | async-done | bytes 1179664 | tf_op jit(solution)/shard_map/all_gather | solution.py:144
  622.2 41.6 %all_gather.75 = bf16[512,768]{1,0:T(8,128)(2,1)S(1)} all-gather(bf16[16,768]{1,0:T(8,128)(2,1)S(1)} %multiply_convert_fusion.6), channel_id=1, replica_groups=mesh['blk'=32] {'blk'}, dimensions={0}, use_global_device_ids=true | all-gather | bytes 811008 | tf_op jit(solution)/shard_map/all_gather | solution.py:181
  663.9 38.8 %all_gather.74 = bf16[512,768]{1,0:T(8,128)(2,1)S(1)} all-gather(bf16[16,768]{1,0:T(8,128)(2,1)S(1)} %multiply_convert_fusion.4), channel_id=1, replica_groups=mesh['blk'=32] {'blk'}, dimensions={0}, use_global_device_ids=true | all-gather | bytes 811008 | tf_op jit(solution)/shard_map/all_gather | solution.py:186
  703.4 36.9 %all-reduce.6 = f32[512]{0:T(512)S(1)} all-reduce(f32[512]{0:T(512)S(1)} %add_dynamic-update-slice_fusion), channel_id=1, replica_groups=mesh['blk'=32] {'blk'}, use_global_device_ids=true, to_apply=%add.6 | all-reduce | flops 512 | bytes 4096
  747.4 8.5 convert_reduce_fusion.1
  761.7 2.5 convolution_convert_fusion.4
  764.3 2.7 reshape.236
  769.5 3.7 fusion.34
  773.2 2.7 copy.125
  775.8 2.5 reshape.209
  778.3 2.6 multiply_reduce_fusion.2
  782.3 2.6 fusion.36
  789.6 2.6 fusion.35
  799.1 4.8 fusion.95
  804.6 6.5 fusion.98
  811.5 7.7 fusion.70
  820.5 3.4 fusion.63
  823.9 42.9 %all-reduce.10 = (f32[1536]{0:T(1024)S(1)}, f32[1536]{0:T(1024)S(1)}, f32[3840]{0:T(1024)S(1)}) all-reduce(f32[1536]{0:T(1024)S(1)} %pad_maximum_fusion.1, f32[1536]{0:T(1024)S(1)} %pad_maximum_fusion.2, f32[3840]{0:T(1024)S(1)} %pad_maximum_fusion), channel_id=2, replica_groups=mesh['blk'=32] {'blk'}, use_global_device_ids=true, to_apply=%region_29.30.clone | all-reduce | flops 6912 | bytes 55296
  869.8 80.1 %reduce-scatter.8.cloned.1.call-done = f32[24,768]{1,0:T(8,128)} async-done(((f32[768,768]{1,0:T(8,128)}), f32[24,768]{1,0:T(8,128)}) %reduce-scatter.8.cloned.1.call-update) | async-done | bytes 73744 | tf_op jit(solution)/shard_map/reduce_scatter | solution.py:266
  949.9 124.4 %reduce-scatter.6.cloned.1.call-done = f32[24,2304]{1,0:T(8,128)} async-done(((f32[768,2304]{1,0:T(8,128)}), f32[24,2304]{1,0:T(8,128)}) %reduce-scatter.6.cloned.1.call-update) | async-done | bytes 221200 | tf_op jit(solution)/shard_map/reduce_scatter | solution.py:265
  1074.3 142.3 %reduce-scatter.10.cloned.1.call-done = f32[24,3072]{1,0:T(8,128)} async-done(((f32[768,3072]{1,0:T(8,128)}), f32[24,3072]{1,0:T(8,128)}) %reduce-scatter.10.cloned.1.call-update) | async-done | bytes 294928 | tf_op jit(solution)/shard_map/reduce_scatter | solution.py:267
  1216.6 141.0 %reduce-scatter.12.cloned.1.call-done = f32[96,768]{1,0:T(8,128)} async-done(((f32[3072,768]{1,0:T(8,128)}), f32[96,768]{1,0:T(8,128)}) %reduce-scatter.12.cloned.1.call-update) | async-done | bytes 294928 | tf_op jit(solution)/shard_map/reduce_scatter | solution.py:268
  (219 shorter events, 76.4 us)
Async XLA Ops:
  7.2 58.7 %copy-start.7 = (bf16[800,768]{1,0:T(8,128)(2,1)S(1)}, bf16[800,768]{1,0:T(8,128)(2,1)}, u32[]{:S(2)}) copy-start(bf16[800,768]{1,0:T(8,128)(2,1)} %param.24) | copy-start | bytes 3686404
  7.2 59.3 %copy-start = (bf16[256,768]{1,0:T(8,128)(2,1)S(1)}, bf16[256,768]{1,0:T(8,128)(2,1)}, u32[]{:S(2)}) copy-start(bf16[256,768]{1,0:T(8,128)(2,1)} %param.21) | copy-start | bytes 1179652
  7.2 59.7 %copy-start.20 = (s32[4,64]{1,0:T(4,128)S(1)}, s32[4,64]{1,0:T(4,128)}, u32[]{:S(2)}) copy-start(s32[4,64]{1,0:T(4,128)} %param.22) | copy-start | bytes 3076
  7.2 61.9 %copy-start.33 = (s32[16]{0:T(128)S(1)}, s32[16]{0:T(128)}, u32[]{:S(2)}) copy-start(s32[16]{0:T(128)} %param.23) | copy-start | bytes 196
  7.2 67.0 %all-gather.21.cloned.1.call-start = ((), (), s32[]{:S(2)}) async-start(), calls=%async_computation.10 | async-start | bytes 3649536 | tf_op jit(solution)/shard_map/all_gather | solution.py:131
  8.0 122.0 %all-gather.23.cloned.1.call-start = ((), (), s32[]{:S(2)}) async-start(), calls=%async_computation.11 | async-start | bytes 1216512 | tf_op jit(solution)/shard_map/all_gather | solution.py:132
  8.7 183.2 %all-gather.11.cloned.1.call-start = ((), (), s32[]{:S(2)}) async-start(), calls=%async_computation.5 | async-start | bytes 3649536 | tf_op jit(solution)/shard_map/all_gather | solution.py:139
  9.4 238.1 %all-gather.13.cloned.1.call-start = ((), (), s32[]{:S(2)}) async-start(), calls=%async_computation.6 | async-start | bytes 1216512 | tf_op jit(solution)/shard_map/all_gather | solution.py:140
  10.0 302.9 %all-gather.25.cloned.1.call-start = ((), (), s32[]{:S(2)}) async-start(), calls=%async_computation.12 | async-start | bytes 4866048 | tf_op jit(solution)/shard_map/all_gather | solution.py:133
  10.6 367.5 %all-gather.27.cloned.1.call-start = ((), (), s32[]{:S(2)}) async-start(), calls=%async_computation.13 | async-start | bytes 4866048 | tf_op jit(solution)/shard_map/all_gather | solution.py:134
  11.2 422.7 %all-gather.29.cloned.1.call-start = ((), (), s32[]{:S(2)}) async-start(), calls=%async_computation.14 | async-start | bytes 1216512 | tf_op jit(solution)/shard_map/all_gather | solution.py:136
  11.9 487.5 %all-gather.15.cloned.1.call-start = ((), (), s32[]{:S(2)}) async-start(), calls=%async_computation.7 | async-start | bytes 4866048 | tf_op jit(solution)/shard_map/all_gather | solution.py:141
  12.7 552.1 %all-gather.17.cloned.1.call-start = ((), (), s32[]{:S(2)}) async-start(), calls=%async_computation.8 | async-start | bytes 4866048 | tf_op jit(solution)/shard_map/all_gather | solution.py:142
  13.4 607.0 %all-gather.19.cloned.1.call-start = ((), (), s32[]{:S(2)}) async-start(), calls=%async_computation.9 | async-start | bytes 1216512 | tf_op jit(solution)/shard_map/all_gather | solution.py:144
  14.0 855.8 %reduce-scatter.14.cloned.1.call-start = ((), (), s32[]{:S(2)}) async-start(), calls=%async_computation.19 | async-start | bytes 2433024 | tf_op jit(solution)/shard_map/reduce_scatter | solution.py:270
  66.6 125.3 %copy-start.16 = (f32[256]{0:T(256)}, f32[256]{0:T(256)S(1)}, u32[]{:S(2)}) copy-start(f32[256]{0:T(256)S(1)} %broadcast_multiply_fusion.7) | copy-start | bytes 3076
  66.9 125.0 %copy-start.21 = (f32[256]{0:T(256)}, f32[256]{0:T(256)S(1)}, u32[]{:S(2)}) copy-start(f32[256]{0:T(256)S(1)} %add_rsqrt_fusion.3) | copy-start | bytes 3076
  67.8 13.3 copy-start.31
  102.2 4.0 copy-start.6
  118.3 73.6 %copy-start.1 = (bf16[256,768]{1,0:T(8,128)(2,1)S(1)}, bf16[256,768]{1,0:T(8,128)(2,1)}, u32[]{:S(2)}) copy-start(bf16[256,768]{1,0:T(8,128)(2,1)} %param.21) | copy-start | bytes 1179652
  133.3 61.8 %copy-start.23 = (f32[800]{0:T(1024)}, f32[800]{0:T(1024)S(1)}, u32[]{:S(2)}) copy-start(f32[800]{0:T(1024)S(1)} %broadcast_multiply_fusion) | copy-start | bytes 9604
  196.3 3.9 copy-start.2
  197.9 6.7 copy-start.4
  206.3 171.8 %copy-start.24 = (f32[800]{0:T(1024)S(1)}, f32[800]{0:T(1024)}, u32[]{:S(2)}) copy-start(f32[800]{0:T(1024)} %copy-done.23) | copy-start | bytes 9604
  206.4 171.8 %copy-start.29 = (f32[3072]{0:T(1024)S(1)}, f32[3072]{0:T(1024)}, u32[]{:S(2)}) copy-start(f32[3072]{0:T(1024)} %slice_convert_fusion) | copy-start | bytes 36868
  206.4 171.8 %copy-start.36 = (f32[768]{0:T(1024)S(1)}, f32[768]{0:T(1024)}, u32[]{:S(2)}) copy-start(f32[768]{0:T(1024)} %slice_convert_fusion.2) | copy-start | bytes 9220
  206.4 171.7 %copy-start.37 = (f32[800]{0:T(1024)S(1)}, f32[800]{0:T(1024)}, u32[]{:S(2)}) copy-start(f32[800]{0:T(1024)} %add_rsqrt_fusion) | copy-start | bytes 9604
  206.4 171.7 %copy-start.40 = (f32[768]{0:T(1024)S(1)}, f32[768]{0:T(1024)}, u32[]{:S(2)}) copy-start(f32[768]{0:T(1024)} %get-tuple-element.42) | copy-start | bytes 9220
  206.4 171.7 %copy-start.41 = (f32[768]{0:T(1024)S(1)}, f32[768]{0:T(1024)}, u32[]{:S(2)}) copy-start(f32[768]{0:T(1024)} %get-tuple-element.77) | copy-start | bytes 9220
  206.9 186.4 %copy-start.8 = (bf16[256,768]{0,1:T(8,128)(2,1)}, bf16[256,768]{0,1:T(8,128)(2,1)S(1)}, u32[]{:S(2)}) copy-start(bf16[256,768]{0,1:T(8,128)(2,1)S(1)} %convert_element_type.148) | copy-start | bytes 1179652
  249.4 506.5 %copy-start.18 = (f32[256]{0:T(256)}, f32[256]{0:T(256)S(1)}, u32[]{:S(2)}) copy-start(f32[256]{0:T(256)S(1)} %broadcast_multiply_fusion.6) | copy-start | bytes 3076
  249.6 506.2 %copy-start.26 = (f32[256]{0:T(256)}, f32[256]{0:T(256)S(1)}, u32[]{:S(2)}) copy-start(f32[256]{0:T(256)S(1)} %add_rsqrt_fusion.2) | copy-start | bytes 3076
  396.2 103.2 %copy-start.28 = (f32[3072]{0:T(1024)S(1)}, f32[3072]{0:T(1024)}, u32[]{:S(2)}) copy-start(f32[3072]{0:T(1024)} %slice_convert_fusion.1) | copy-start | bytes 36868
  499.4 65.4 %copy-start.35 = (f32[768]{0:T(1024)S(1)}, f32[768]{0:T(1024)}, u32[]{:S(2)}) copy-start(f32[768]{0:T(1024)} %slice_convert_fusion.7) | copy-start | bytes 9220
  504.9 65.9 %copy-start.32 = (s32[256]{0:T(256)S(1)}, s32[256]{0:T(256)}, u32[]{:S(2)}) copy-start(s32[256]{0:T(256)} %copy-done.31) | copy-start | bytes 3076
  504.9 65.9 %copy-start.42 = (f32[16]{0:T(128)S(1)}, f32[16]{0:T(128)}, u32[]{:S(2)}) copy-start(f32[16]{0:T(128)} %convert_reduce_fusion.3) | copy-start | bytes 196
  571.3 170.3 %copy-start.34 = (s32[16]{0:T(128)S(1)}, s32[16]{0:T(128)}, u32[]{:S(2)}) copy-start(s32[16]{0:T(128)} %param.23) | copy-start | bytes 196
  744.7 205.3 %reduce-scatter.8.cloned.1.call-start = ((), (), s32[]{:S(2)}) async-start(), calls=%async_computation.16 | async-start | bytes 2433024 | tf_op jit(solution)/shard_map/reduce_scatter | solution.py:266
  746.4 9.5 slice-start
  747.4 8.5 slice-start.1
  761.7 312.7 %reduce-scatter.6.cloned.1.call-start = ((), (), s32[]{:S(2)}) async-start(), calls=%async_computation.15 | async-start | bytes 7299072 | tf_op jit(solution)/shard_map/reduce_scatter | solution.py:265
  778.3 2.6 copy-start.15
  803.9 412.7 %reduce-scatter.10.cloned.1.call-start = ((), (), s32[]{:S(2)}) async-start(), calls=%async_computation.17 | async-start | bytes 9732096 | tf_op jit(solution)/shard_map/reduce_scatter | solution.py:267
  811.2 546.5 %reduce-scatter.12.cloned.1.call-start = ((), (), s32[]{:S(2)}) async-start(), calls=%async_computation.18 | async-start | bytes 9732096 | tf_op jit(solution)/shard_map/reduce_scatter | solution.py:268
  820.4 3.4 copy-start.39
  820.4 3.4 copy-start.38
  820.5 3.4 copy-start.25
  820.5 3.4 copy-start.30
  (12 other events, 16.3 us)
Sparse Core Ops, SparseCore 0:
  11.0 63.2 all-gather.20
  77.1 52.8 all-gather.22
  132.9 58.9 all-gather.10
  194.6 52.8 all-gather.12
  250.3 62.5 all-gather.24
  315.6 62.4 all-gather.26
  381.0 52.8 all-gather.28
  436.8 62.5 all-gather.14
  502.3 62.4 all-gather.16
  567.5 52.8 all-gather.18
  744.8 100.5 reduce-scatter.13
  851.9 97.9 reduce-scatter.7
  956.2 118.0 reduce-scatter.5
  1081.7 134.9 reduce-scatter.9
  1222.9 134.6 reduce-scatter.11
where the time goes:
time: 1380 us; the launch traced here: 1360 us
  waiting for transfers between devices  943 us (68%)
  blocking collectives  203 us (15%)
  matrix products  112 us (8%)
  local copies, waits for them, and re-layouts  66.6 us (5%)
  other arithmetic  22.5 us (2%)
  between operations  15.7 us (1%)
    reduce_scatter x1, waiting for transfers between devices, on_device(): lax.psum_scatter(grad_in, 'blk', scatter_dimension=0, tiled=True)  142 us
    reduce_scatter x1, waiting for transfers between devices, on_device(): lax.psum_scatter(grad_down, 'blk', scatter_dimension=0, tiled=True)  141 us
    reduce_scatter x1, waiting for transfers between devices, on_device(): lax.psum_scatter(grad_qkv, 'blk', scatter_dimension=0, tiled=True)  124 us
    unnamed x3, blocking collectives  123 us
    reduce_scatter x1, waiting for transfers between devices, on_device(): lax.psum_scatter(grad_out, 'blk', scatter_dimension=0, tiled=True)  80.1 us
    all_gather x1, waiting for transfers between devices, on_device(): lax.all_gather(img_down, 'blk', axis=0, tiled=True)  65.2 us
    all_gather x1, waiting for transfers between devices, on_device(): lax.all_gather(txt_in, 'blk', axis=0, tiled=True)  63.8 us
    all_gather x1, waiting for transfers between devices, on_device(): lax.all_gather(img_in, 'blk', axis=0, tiled=True)  63.2 us
  transfers between devices with their start and end apart: 15, of which 14 were waited for; matrix products, arithmetic and copies ran while one was open for 14% of the time, Pallas kernels for 0%

commit v1 on v0

v1 whole, which is shorter than its diff:
```python
import jax
import jax.numpy as jnp
from jax import lax
from jax.sharding import PartitionSpec as P

HEAD = 64
PATCHES = 50
CAPS = 4
TILE = 512

HIGH = lax.Precision.HIGHEST
F32 = jnp.float32
BF16 = jnp.bfloat16


def gelu(z):
    return 0.5 * z * (1.0 + jnp.tanh(0.7978845608028654 * (z + 0.044715 * z * z * z)))


def normalize(x):
    mean = jnp.mean(x, axis=-1, keepdims=True)
    cent = x - mean
    rstd = lax.rsqrt(jnp.mean(cent * cent, axis=-1, keepdims=True) + 1e-06)
    return (cent * rstd, rstd)


def norm_back(grad, normed, rstd):
    return rstd * (
        grad
        - jnp.mean(grad, axis=-1, keepdims=True)
        - normed * jnp.mean(grad * normed, axis=-1, keepdims=True)
    )


def matmul(left, right):
    return jnp.dot(left, right, preferred_element_type=F32)


def left_product(left, right):
    return lax.dot_general(left, right, (((0,), (0,)), ((), ())), preferred_element_type=F32)


def right_product(left, right):
    return lax.dot_general(left, right, (((1,), (1,)), ((), ())), preferred_element_type=F32)


def attention(qkv, same):
    groups, length, triple = qkv.shape
    width = triple // 3
    heads = width // HEAD
    query = qkv[..., :width].reshape(groups, length, heads, HEAD)
    keys = qkv[..., width : 2 * width].reshape(groups, length, heads, HEAD)
    values = qkv[..., 2 * width :].reshape(groups, length, heads, HEAD)
    scores = jnp.einsum("gthd,gshd->ghts", query, keys, preferred_element_type=F32) * 0.125
    scores = jnp.where(same[:, None], scores, -1000000000.0)
    top = jnp.max(scores, axis=-1, keepdims=True)
    expo = jnp.exp(scores - top)
    probs = expo / jnp.sum(expo, axis=-1, keepdims=True)
    mixed = jnp.einsum("ghts,gshd->gthd", probs.astype(BF16), values, preferred_element_type=F32)
    return (mixed.reshape(groups * length, width).astype(BF16), probs, query, keys, values)


def forward_block(x, same, groups, gains, shifts, w_qkv, w_out, w_in, biases):
    width = x.shape[1]
    units = w_in.shape[1]
    normed1, rstd1 = normalize(x)
    act1 = (normed1 * gains[:width] + shifts[:width]).astype(BF16)
    qkv = matmul(act1, w_qkv).astype(BF16).reshape(groups, -1, 3 * width)
    mixed, probs, query, keys, values = attention(qkv, same)
    second = x + matmul(mixed, w_out)
    normed2, rstd2 = normalize(second)
    act2 = (normed2 * gains[width:] + shifts[width:]).astype(BF16)
    inner = matmul(act2, w_in) + biases[:units]
    hidden = gelu(inner).astype(BF16)
    return (second, hidden, (normed1, rstd1, act1, probs, query, keys, values, mixed, normed2, rstd2, act2, inner))


def pack(w_qkv, w_out, w_in, w_down, w_proj, vectors):
    rows = w_qkv.shape[0]
    down = w_down.reshape(-1, rows, w_down.shape[1])
    block = jnp.pad(vectors, (0, rows * 128 - vectors.shape[0])).reshape(rows, 128)
    return jnp.concatenate([w_qkv, w_out, w_in, w_proj, *down, block], axis=1)


def unpack(whole, devices, width, units):
    rows = width // devices
    cuts = [3 * width, 4 * width, 4 * width + units, 5 * width + units]
    down = whole[:, cuts[3] : cuts[3] + units]
    down = down.reshape(devices, rows, units // width, width).transpose(0, 2, 1, 3).reshape(units, width)
    vectors = whole[:, cuts[3] + units :].reshape(devices, rows * 128)
    return (
        whole[:, : cuts[0]],
        whole[:, cuts[0] : cuts[1]],
        whole[:, cuts[1] : cuts[2]],
        down,
        whole[:, cuts[2] : cuts[3]],
        vectors,
    )


def gather(part):
    return lax.all_gather(part, "blk", axis=0, tiled=True)


def split_vectors(vectors, sizes):
    parts = []
    start = 0
    for size in sizes:
        parts.append(vectors[:, start : start + size].reshape(-1))
        start += size
    return parts


def head_tile(proj, factor, image_emb, scale, row_lse, col_lse, pairs, sim):
    hit = pairs[:, None] == jnp.arange(image_emb.shape[0], dtype=jnp.int32)[None, :]
    weights_sim = (
        0.5 * jnp.exp(sim - row_lse[:, None]) + 0.5 * jnp.exp(sim - col_lse[None, :]) - hit.astype(F32)
    )
    d_emb = scale * matmul(weights_sim.astype(BF16), image_emb)
    d_proj = factor * d_emb - proj * (factor * factor * factor) * jnp.sum(d_emb * proj, axis=-1, keepdims=True)
    pos = jnp.sum(jnp.where(hit, sim, 0.0), axis=1)
    pair_col = jnp.sum(jnp.where(hit, col_lse[None, :], 0.0), axis=1)
    return (d_proj.astype(BF16), 0.5 * (row_lse - pos) + 0.5 * (pair_col - pos))


def unit_rows(proj):
    factor = lax.rsqrt(jnp.sum(proj * proj, axis=-1, keepdims=True) + 1e-06)
    return (proj * factor, factor)


def on_device(devices, *args):
    (
        text_tokens,
        segment_ids,
        pair_index,
        image_tokens,
        logit_scale,
        img_gains,
        img_shifts,
        img_qkv,
        img_out,
        img_in,
        img_down,
        img_biases,
        img_proj,
        txt_gains,
        txt_shifts,
        txt_qkv,
        txt_out,
        txt_in,
        txt_down,
        txt_biases,
        txt_proj,
    ) = args
    width = text_tokens.shape[1]
    units = img_in.shape[1]
    scale = logit_scale[0]
    rows, length = segment_ids.shape
    tokens = rows * length
    captions = pair_index.shape[0]
    images = image_tokens.shape[0] // PATCHES
    device = lax.axis_index("blk")

    caption_of = (jnp.arange(rows, dtype=jnp.int32)[:, None] * CAPS + segment_ids).reshape(tokens)
    member = (jnp.arange(captions, dtype=jnp.int32)[:, None] == caption_of[None, :]).astype(F32)
    counts = jnp.sum(member, axis=1)

    vec = (width * 2 // devices, width * 2 // devices, (units + width) // devices)
    image_whole = gather(
        pack(img_qkv, img_out, img_in, img_down, img_proj, jnp.concatenate([img_gains, img_shifts, img_biases]))
    )
    text_vectors = jnp.concatenate(
        [
            txt_gains,
            txt_shifts,
            txt_biases,
            (pair_index // 64).astype(BF16),
            (pair_index % 64).astype(BF16),
            counts.astype(BF16),
        ]
    )
    text_whole = gather(pack(txt_qkv, txt_out, txt_in, txt_down, txt_proj, text_vectors))

    w_qkv, w_out, w_in, w_down, w_proj, vectors = unpack(image_whole, devices, width, units)
    gains, shifts, biases = split_vectors(vectors, vec)
    every = jnp.ones((images, PATCHES, PATCHES), jnp.bool_)
    second, hidden, unused = forward_block(
        image_tokens.astype(F32), every, images, gains, shifts, w_qkv, w_out, w_in, biases
    )
    image_y = second + matmul(hidden, w_down) + biases[units:]
    image_pool = jnp.mean(image_y.reshape(images, PATCHES, width), axis=1).astype(BF16)
    image_proj = w_proj

    w_qkv, w_out, w_in, w_down, w_proj, vectors = unpack(text_whole, devices, width, units)
    gains, shifts, biases, pair_hi, pair_lo, every_count = split_vectors(vectors, vec + (captions,) * 3)
    every_pair = pair_hi.astype(jnp.int32) * 64 + pair_lo.astype(jnp.int32)
    same = segment_ids[:, :, None] == segment_ids[:, None, :]
    x = text_tokens.astype(F32)
    second, hidden, kept = forward_block(x, same, rows, gains, shifts, w_qkv, w_out, w_in, biases)
    y = second + matmul(hidden, w_down) + biases[units:]
    normed1, rstd1, act1, probs, query, keys, values, mixed, normed2, rstd2, act2, inner = kept
    text_out = y.astype(BF16)
    share = member / counts[:, None]
    pool_low = jnp.dot(share, y, precision=HIGH, preferred_element_type=F32).astype(BF16)
    hidden_sum = jnp.dot(member, hidden.astype(F32), precision=HIGH, preferred_element_type=F32).astype(BF16)
    hidden_sum = lax.all_to_all(hidden_sum, "blk", split_axis=1, concat_axis=0, tiled=True)

    pools = gather(jnp.concatenate([image_pool, pool_low])).reshape(devices, 2, captions, width)
    image_emb = unit_rows(matmul(pools[:, 0].reshape(-1, width), image_proj))[0].astype(BF16)
    pool_all = pools[:, 1].reshape(-1, width)
    total = pool_all.shape[0]
    col_max = jnp.full((total,), -1e30, F32)
    col_sum = jnp.zeros((total,), F32)
    held = []
    for start in range(0, total, TILE):
        proj = matmul(pool_all[start : start + TILE], w_proj)
        unit, factor = unit_rows(proj)
        sim = scale * right_product(unit.astype(BF16), image_emb)
        top = jnp.max(sim, axis=1)
        row_lse = top + jnp.log(jnp.sum(jnp.exp(sim - top[:, None]), axis=1))
        new_max = jnp.maximum(col_max, jnp.max(sim, axis=0))
        col_sum = col_sum * jnp.exp(col_max - new_max) + jnp.sum(jnp.exp(sim - new_max[None, :]), axis=0)
        col_max = new_max
        held.append((proj, factor, row_lse, sim))
    col_lse = col_max + jnp.log(col_sum)
    d_proj = []
    losses = []
    for start, (proj, factor, row_lse, sim) in zip(range(0, total, TILE), held):
        grad, loss = head_tile(
            proj, factor, image_emb, scale, row_lse, col_lse, every_pair[start : start + TILE], sim
        )
        d_proj.append(grad)
        losses.append(loss)
    d_proj = jnp.concatenate(d_proj)
    pair_loss = lax.dynamic_slice_in_dim(jnp.concatenate(losses), device * captions, captions)
    own = width // devices
    grad_proj = left_product(lax.dynamic_slice_in_dim(pool_all, device * own, own, axis=1), d_proj)
    d_each = right_product(d_proj, w_proj) / every_count.astype(F32)[:, None]
    grad_down = left_product(hidden_sum, d_each.astype(BF16))
    d_mine = lax.dynamic_slice_in_dim(d_each, device * captions, captions)

    d_y = lax.dot_general(member, d_mine, (((0,), (0,)), ((), ())), precision=HIGH, preferred_element_type=F32)
    grad_outer = jnp.sum(d_y, axis=0)
    d_hidden = right_product(d_mine.astype(BF16), w_down)
    d_hidden = lax.dot_general(member, d_hidden, (((0,), (0,)), ((), ())), precision=HIGH, preferred_element_type=F32)
    unused_value, gelu_pull = jax.vjp(gelu, inner)
    d_inner = gelu_pull(d_hidden)[0].astype(BF16)
    grad_in = left_product(act2, d_inner)
    grad_inner = jnp.sum(d_inner.astype(F32), axis=0)
    grad_biases = jnp.concatenate([grad_inner, grad_outer])
    d_act2 = right_product(d_inner, w_in)
    gain2 = jnp.sum(d_act2 * normed2, axis=0)
    shift2 = jnp.sum(d_act2, axis=0)
    d_second = d_y + norm_back(d_act2 * gains[width:], normed2, rstd2)
    d_second_low = d_second.astype(BF16)
    grad_out = left_product(mixed, d_second_low)
    d_mixed = right_product(d_second_low, w_out).astype(BF16).reshape(rows, length, width // HEAD, HEAD)
    probs_low = probs.astype(BF16)
    d_values = jnp.einsum("ghts,gthd->gshd", probs_low, d_mixed, preferred_element_type=F32)
    d_probs = jnp.einsum("gthd,gshd->ghts", d_mixed, values, preferred_element_type=F32)
    d_scores = (probs * (d_probs - jnp.sum(probs * d_probs, axis=-1, keepdims=True))).astype(BF16)
    d_query = 0.125 * jnp.einsum("ghts,gshd->gthd", d_scores, keys, preferred_element_type=F32)
    d_keys = 0.125 * jnp.einsum("ghts,gthd->gshd", d_scores, query, preferred_element_type=F32)
    d_qkv = jnp.concatenate(
        [d_query.reshape(tokens, width), d_keys.reshape(tokens, width), d_values.reshape(tokens, width)], axis=1
    ).astype(BF16)
    grad_qkv = left_product(act1, d_qkv)
    d_act1 = right_product(d_qkv, w_qkv)
    gain1 = jnp.sum(d_act1 * normed1, axis=0)
    shift1 = jnp.sum(d_act1, axis=0)
    text_grad = d_second + norm_back(d_act1 * gains[:width], normed1, rstd1)
    sums = jnp.concatenate(
        [
            jnp.concatenate([gain1, gain2]).reshape(devices, -1),
            jnp.concatenate([shift1, shift2]).reshape(devices, -1),
            grad_biases.reshape(devices, -1),
        ],
        axis=1,
    )
    used = sums.shape[1]
    sums = jnp.pad(sums, ((0, 0), (0, own * 128 - used))).reshape(width, 128)
    mine = lax.psum_scatter(
        jnp.concatenate([grad_qkv, grad_out, grad_in, sums], axis=1).astype(BF16),
        "blk",
        scatter_dimension=0,
        tiled=True,
    ).astype(F32)
    sums = mine[:, 4 * width + units :].reshape(-1)
    return (
        pair_loss,
        text_out,
        text_grad,
        sums[: vec[0]],
        sums[vec[0] : vec[0] + vec[1]],
        mine[:, : 3 * width],
        mine[:, 3 * width : 4 * width],
        mine[:, 4 * width : 4 * width + units],
        grad_down,
        sums[vec[0] + vec[1] : used],
        grad_proj,
    )


def solution(mesh):
    devices = mesh.shape["blk"]
    row = P("blk", None)
    flat = P("blk")
    tower = (flat, flat, row, row, row, row, flat, row)

    def body(*args):
        return on_device(devices, *args)

    return jax.shard_map(
        body,
        mesh=mesh,
        in_specs=(row, row, flat, row, P()) + tower + tower,
        out_specs=(flat, row, row, flat, flat, row, row, row, row, flat, row),
        check_vma=False,
    )
```

time: 1380 us -> 660 us (0.48)
  waiting for transfers between devices: 943 us -> 374 us
  blocking collectives: 203 us -> 0 us
  local copies, waits for them, and re-layouts: 66.6 us -> 121 us
    reduce_scatter x5 -> x0, waiting for transfers between devices: 488 us -> none  [the longest x1 142 us: on_device(): lax.psum_scatter(grad_in, 'blk', scatter_dimension=0, tiled=True)]
    all_gather x10 -> x3, waiting for transfers between devices: 449 us -> 258 us  [gather(): return lax.all_gather(part, 'blk', axis=0, tiled=True)]
    unnamed x3 -> x0, blocking collectives: 123 us -> none
    unnamed x15 -> x5, waiting for transfers between devices: 6.32 us -> 112 us
    all_gather x2 -> x0, blocking collectives: 80.4 us -> none  [the longest x1 41.6 us: on_device(): lax.all_gather(caption_emb, 'blk', axis=0, tiled=True)]
    reshape x4 -> x13, local copies, waits for them, and re-layouts: 13.1 us -> 33 us  [the longest x2 19.7 us: unpack(): down.reshape(devices, rows, units // width, width).transpose(0, 2, 1, 3)]
    slice x0 -> x12, local copies, waits for them, and re-layouts: none -> 18.9 us  [the longest x2 9.58 us: unpack(): down = whole[:, cuts[3]:cuts[3] + units]]
    dot_general x19 -> x22, matrix products: 66.7 us -> 68.2 us  [the longest x11 44.2 us: matmul(): return jnp.dot(left, right, preferred_element_type=F32)]
  transfers between devices with their start and end apart: 15 -> 5, of which waited for: 14 -> 5; matrix products, arithmetic and copies ran while one was open for 14% -> 4% of each run, Pallas kernels for 0% -> 0%
where the time goes in v1:
time: 660 us; the launch traced here: 647 us
  waiting for transfers between devices  374 us (57%)
  local copies, waits for them, and re-layouts  121 us (18%)
  matrix products  101 us (15%)
  other arithmetic  32.1 us (5%)
  between operations  15.6 us (2%)
    all_gather x3, waiting for transfers between devices, gather(): return lax.all_gather(part, 'blk', axis=0, tiled=True)  258 us
    unnamed x5, waiting for transfers between devices  112 us
    dot_general x11, matrix products, matmul(): return jnp.dot(left, right, preferred_element_type=F32)  44.2 us
    unnamed x116, local copies, waits for them, and re-layouts  22.5 us
    reshape x2, local copies, waits for them, and re-layouts, unpack(): down.reshape(devices, rows, units // width, width).transpose(0, 2, 1, 3)  19.7 us
    dot_general x6, matrix products, right_product(): lax.dot_general(left, right, (((1,), (1,)), ((), ())), preferred_element_...  17.6 us
  transfers between devices with their start and end apart: 5, of which 5 were waited for; matrix products, arithmetic and copies ran while one was open for 4% of the time, Pallas kernels for 0%

profile of v1, /device:TPU:0, one launch (start us, length us, event | category | flops | bytes accessed | tf_op | source)
XLA Modules:
  0.0 647.3 jit_solution(5691081464603512392)
XLA Ops:
  17.6 2.1 concatenate.51
  29.5 98.0 %all-gather.4.cloned.1.call-done = bf16[768,10112]{1,0:T(8,128)(2,1)} async-done(((bf16[24,10112]{1,0:T(8,128)(2,1)}), bf16[768,10112]{1,0:T(8,128)(2,1)}) %all-gather.4.cloned.1.call-update) | async-done | bytes 15532048 | tf_op jit(solution)/shard_map/all_gather | solution.py:102
  129.9 108.4 %all-gather.6.cloned.1.call-done = bf16[768,10112]{1,0:T(8,128)(2,1)} async-done(((bf16[24,10112]{1,0:T(8,128)(2,1)}), bf16[768,10112]{1,0:T(8,128)(2,1)}) %all-gather.6.cloned.1.call-update) | async-done | bytes 15532048 | tf_op jit(solution)/shard_map/all_gather | solution.py:102
  241.0 6.9 %convolution_convert_fusion = bf16[800,2304]{1,0:T(8,128)(2,1)} fusion(bf16[768,10112]{1,0:T(8,128)(2,1)} %all-gather.4.cloned.1.call-done, bf16[800,768]{1,0:T(8,128)(2,1)S(1)} %copy-done.11, f32[768]{0:T(1024)S(1)} %reshape.388, f32[768]{0:T(1024)S(1)} %reshape.387, f32[800]{0:T(1024)S(1)} %add_rsqrt_fusion.1, f32[800]{0:T(1024)S(1)} %broadcast_multiply_fusion.1), kind=kOutput, calls=%fused_computation.11 | convolution fusion | flops 2836684800 | bytes 8466688 | tf_op jit(solution)/shard_map/dot_general | solution.py:36
  247.8 4.9 reshape.362
  252.8 4.2 fusion.127
  257.0 3.5 reshape.397
  260.5 4.8 reshape.398
  265.4 3.5 fusion.31
  268.9 4.0 fusion.134
  272.9 3.2 reshape.396
  276.1 5.2 convert_bitcast_fusion
  281.8 2.9 convert_element_type.257
  284.7 3.3 fusion.135
  288.6 4.8 slice.219
  293.3 10.0 %reshape.367 = bf16[32,24,4,768]{3,2,1,0:T(4,128)(2,1)} reshape(bf16[768,3072]{1,0:T(8,128)(2,1)} %slice.219) | data formatting | bytes 9437184 | tf_op jit(solution)/shard_map/reshape | solution.py:89
  303.3 3.3 copy.145
  306.6 7.9 %fusion.6 = bf16[800,3072]{1,0:T(8,128)(2,1)S(1)} fusion(f32[3072]{0:T(1024)S(1)} %copy-done.41, bf16[768,10112]{1,0:T(8,128)(2,1)} %all-gather.4.cloned.1.call-done, f32[800,768]{1,0:T(8,128)S(1)} %get-tuple-element.59, f32[768]{0:T(1024)S(1)} %reshape.390, f32[768]{0:T(1024)S(1)} %reshape.389, f32[800]{0:T(1024)S(1)} %add_rsqrt_fusion, ...), kind=kOutput, calls=%fused_computation.7 | convolution fusion | flops 3802521600 | bytes 12116224 | tf_op jit(solution)/shard_map/dot_general | solution.py:36
  314.5 5.4 add_add_fusion
  319.9 2.2 reshape.369
  323.2 3.2 convolution_convert_fusion.3
  331.6 2.4 fusion.45
  335.1 2.0 fusion.133
  337.5 4.8 slice.234
  342.3 9.8 %reshape.377 = bf16[32,24,4,768]{3,2,1,0:T(4,128)(2,1)} reshape(bf16[768,3072]{1,0:T(8,128)(2,1)} %slice.234) | data formatting | bytes 9437184 | tf_op jit(solution)/shard_map/reshape | solution.py:89
  352.1 3.3 copy.151
  355.4 7.9 %multiply_convert_fusion = (bf16[256,3072]{1,0:T(8,128)(2,1)S(1)}, f32[256,3072]{1,0:T(8,128)}) fusion(f32[3072]{0:T(1024)S(1)} %copy-done.40, bf16[768,10112]{1,0:T(8,128)(2,1)} %all-gather.6.cloned.1.call-done, f32[256,768]{1,0:T(8,128)S(1)} %get-tuple-element.53, f32[768]{0:T(1024)S(1)} %reshape.394, f32[768]{0:T(1024)S(1)} %reshape.393, ...), kind=kOutput, calls=%fused_computation.38 | convolution fusion | flops 1216806912 | bytes 10244096 | tf_op jit(solution)/shard_map/dot_general | solution.py:36
  363.3 2.1 fusion.136
  367.8 52.1 %all-gather.8.cloned.1.call-done = bf16[1024,768]{1,0:T(8,128)(2,1)} async-done(((bf16[32,768]{1,0:T(8,128)(2,1)}), bf16[1024,768]{1,0:T(8,128)(2,1)}) %all-gather.8.cloned.1.call-update) | async-done | bytes 1572880 | tf_op jit(solution)/shard_map/all_gather | solution.py:102
  421.4 2.4 multiply_reduce_fusion.5
  423.8 2.1 multiply_reduce_fusion.4
  430.5 2.3 convolution_divide_fusion
  435.3 4.8 fusion.137
  440.1 5.2 multiply_reduce_fusion.6
  446.6 2.8 convolution_convert_fusion.8
  452.6 3.6 fusion.46
  456.3 2.3 multiply_reduce_fusion.2
  460.6 3.7 convolution_convert_fusion.1
  470.4 2.3 convolution_convert_fusion.2
  472.8 2.4 copy.166
  477.2 5.1 fusion.79
  491.0 8.3 %pad_maximum_fusion = bf16[768,6272]{1,0:T(8,128)(2,1)} fusion(bf16[768,128]{1,0:T(8,128)(2,1)} %reshape.385, bf16[768,3072]{1,0:T(8,128)(2,1)} %convolution_convert_fusion.1, bf16[768,768]{1,0:T(8,128)(2,1)} %copy.166, bf16[768,2304]{1,0:T(8,128)(2,1)S(1)} %convolution_convert_fusion.2), kind=kLoop, calls=%fused_computation.8 | loop fusion | flops 38535168 | bytes 19267584 | tf_op jit(solution)/shard_map/concatenate | solution.py:283
  500.0 2.5 convolution_convert_fusion.4
  505.8 3.6 all-to-all-start
  511.4 1.9 fusion.101
  514.6 3.0 all-to-all-done
  517.6 1.9 fusion.81
  521.4 112.2 %reduce-scatter.4.cloned.1.call-done = bf16[24,6272]{1,0:T(8,128)(2,1)} async-done(((bf16[768,6272]{1,0:T(8,128)(2,1)}), bf16[24,6272]{1,0:T(8,128)(2,1)}) %reduce-scatter.4.cloned.1.call-update) | async-done | bytes 301072
  (235 shorter events, 83.2 us)
Async XLA Ops:
  7.2 19.9 %copy-start.3 = (bf16[256,768]{1,0:T(8,128)(2,1)S(1)}, bf16[256,768]{1,0:T(8,128)(2,1)}, u32[]{:S(2)}) copy-start(bf16[256,768]{1,0:T(8,128)(2,1)} %param.21) | copy-start | bytes 1179652
  7.2 20.8 %copy-start.11 = (bf16[800,768]{1,0:T(8,128)(2,1)S(1)}, bf16[800,768]{1,0:T(8,128)(2,1)}, u32[]{:S(2)}) copy-start(bf16[800,768]{1,0:T(8,128)(2,1)} %param.24) | copy-start | bytes 3686404
  7.2 120.2 %all-gather.4.cloned.1.call-start = ((), (), s32[]{:S(2)}) async-start(), calls=%async_computation.2 | async-start | bytes 16017408 | tf_op jit(solution)/shard_map/all_gather | solution.py:102
  15.4 14.0 %copy-start.31 = (s32[4,64]{1,0:T(4,128)S(1)}, s32[4,64]{1,0:T(4,128)}, u32[]{:S(2)}) copy-start(s32[4,64]{1,0:T(4,128)} %param.22) | copy-start | bytes 3076
  15.4 222.9 %all-gather.6.cloned.1.call-start = ((), (), s32[]{:S(2)}) async-start(), calls=%async_computation.3 | async-start | bytes 16017408 | tf_op jit(solution)/shard_map/all_gather | solution.py:102
  16.3 1.3 copy-start.35
  27.0 392.9 %all-gather.8.cloned.1.call-start = ((), (), s32[]{:S(2)}) async-start(), calls=%async_computation.4 | async-start | bytes 1622016 | tf_op jit(solution)/shard_map/all_gather | solution.py:102
  268.9 4.0 copy-start.10
  303.3 3.3 copy-start.41
  306.6 7.9 %copy-start.43 = (f32[768]{0:T(1024)S(1)}, f32[768]{0:T(1024)}, u32[]{:S(2)}) copy-start(f32[768]{0:T(1024)} %slice_convert_fusion.12) | copy-start | bytes 9220
  322.2 1.0 copy-start.4
  322.2 1.0 copy-start.30
  322.2 1.0 copy-start.32
  327.2 3.1 copy-start.6
  327.7 1.1 copy-start.8
  335.1 7.2 %copy-start.17 = (bf16[256,768]{0,1:T(8,128)(2,1)}, bf16[256,768]{0,1:T(8,128)(2,1)S(1)}, u32[]{:S(2)}) copy-start(bf16[256,768]{0,1:T(8,128)(2,1)S(1)} %convert_element_type.281) | copy-start | bytes 1179652
  337.4 107.9 %copy-start.38 = (f32[256]{0:T(256)}, f32[256]{0:T(256)S(1)}, u32[]{:S(2)}) copy-start(f32[256]{0:T(256)S(1)} %add_rsqrt_fusion.4) | copy-start | bytes 3076
  352.1 3.3 copy-start.40
  355.4 7.9 %copy-start = (bf16[32,4,24,768]{3,2,1,0:T(8,128)(2,1)}, bf16[32,4,24,768]{3,2,1,0:T(8,128)(2,1)S(1)}, u32[]{:S(2)}) copy-start(bf16[32,4,24,768]{3,2,1,0:T(8,128)(2,1)S(1)} %copy.151) | copy-start | bytes 14155780
  355.4 7.9 %copy-start.42 = (f32[768]{0:T(1024)S(1)}, f32[768]{0:T(1024)}, u32[]{:S(2)}) copy-start(f32[768]{0:T(1024)} %slice_convert_fusion.11) | copy-start | bytes 9220
  363.3 2.2 copy-start.19
  363.3 2.2 copy-start.36
  363.3 2.2 copy-start.45
  366.6 267.0 %reduce-scatter.4.cloned.1.call-start = ((), (), s32[]{:S(2)}) async-start(), calls=%async_computation.5 | async-start | bytes 9934848
  421.4 4.6 copy-start.22
  429.2 3.6 slice-start
  429.5 1.0 copy-start.12
  430.5 2.4 slice-start.1
  432.8 12.5 %copy-start.15 = (f32[512,768]{1,0:T(8,128)}, f32[512,768]{1,0:T(8,128)S(1)}, u32[]{:S(2)}) copy-start(f32[512,768]{1,0:T(8,128)S(1)} %convolution_divide_fusion) | copy-start | bytes 4718596
  432.9 2.5 copy-start.46
  440.1 5.2 copy-start.20
  446.6 17.6 %copy-start.1 = (f32[256,768]{1,0:T(8,128)}, f32[256,768]{1,0:T(8,128)S(1)}, u32[]{:S(2)}) copy-start(f32[256,768]{1,0:T(8,128)S(1)} %get-tuple-element.35) | copy-start | bytes 2359300
  452.6 3.7 copy-start.23
  456.3 2.3 copy-start.9
  458.6 1.1 copy-start.7
  459.1 1.5 copy-start.21
  459.1 1.5 copy-start.39
  460.6 3.7 copy-start.18
  464.2 1.6 copy-start.25
  468.0 2.5 copy-start.33
  469.4 1.0 copy-start.14
  499.3 12.0 %copy-start.13 = (bf16[512,768]{1,0:T(8,128)(2,1)S(1)}, bf16[512,768]{1,0:T(8,128)(2,1)}, u32[]{:S(2)}) copy-start(bf16[512,768]{1,0:T(8,128)(2,1)} %copy-done.12) | copy-start | bytes 2359300
  499.3 18.3 %copy-start.16 = (f32[512,768]{1,0:T(8,128)S(1)}, f32[512,768]{1,0:T(8,128)}, u32[]{:S(2)}) copy-start(f32[512,768]{1,0:T(8,128)} %copy-done.15) | copy-start | bytes 4718596
  500.0 19.6 %copy-start.2 = (f32[256,768]{1,0:T(8,128)S(1)}, f32[256,768]{1,0:T(8,128)}, u32[]{:S(2)}) copy-start(f32[256,768]{1,0:T(8,128)} %copy-done.1) | copy-start | bytes 2359300
  500.0 19.6 %copy-start.5 = (bf16[256,768]{1,0:T(8,128)(2,1)S(1)}, bf16[256,768]{1,0:T(8,128)(2,1)}, u32[]{:S(2)}) copy-start(bf16[256,768]{1,0:T(8,128)(2,1)} %param.21) | copy-start | bytes 1179652
  500.0 19.6 %copy-start.34 = (f32[256]{0:T(256)S(1)}, f32[256]{0:T(256)}, u32[]{:S(2)}) copy-start(f32[256]{0:T(256)} %add_rsqrt_fusion.5) | copy-start | bytes 3076
  505.8 11.8 %all-to-all-start = ((bf16[16,32,96]{2,0,1:T(8,128)(2,1)}), bf16[16,32,96]{2,0,1:T(8,128)(2,1)}, u32[]{:S(2)}, u32[]{:S(2)}) async-start(bf16[16,32,96]{2,0,1:T(8,128)(2,1)} %copy.167), calls=%async_computation | async-start | bytes 262144 | tf_op jit(solution)/shard_map/all_to_all | solution.py:206
  513.3 6.3 copy-start.26
  (6 other events, 4.2 us)
Sparse Core Ops, SparseCore 0:
  15.5 111.8 all-gather.3
  130.9 107.3 all-gather.5
  366.8 53.1 all-gather.7
  499.5 134.0 reduce-scatter.3

commit v2 on v1

v2 whole, which is shorter than its diff:
```python
import functools

import jax
import jax.numpy as jnp
from jax import lax
from jax.experimental import pallas as pl
from jax.experimental.pallas import tpu as pltpu
from jax.sharding import PartitionSpec as P

HEAD = 64
PATCHES = 50
CAPS = 4
TILE = 512
GROUP_PAD = 112

F32 = jnp.float32
BF16 = jnp.bfloat16


def gelu(z):
    return 0.5 * z * (1.0 + jnp.tanh(0.7978845608028654 * (z + 0.044715 * z * z * z)))


def normalize(x):
    mean = jnp.mean(x, axis=-1, keepdims=True)
    cent = x - mean
    rstd = lax.rsqrt(jnp.mean(cent * cent, axis=-1, keepdims=True) + 1e-06)
    return (cent * rstd, rstd)


def norm_back(grad, normed, rstd):
    return rstd * (
        grad
        - jnp.mean(grad, axis=-1, keepdims=True)
        - normed * jnp.mean(grad * normed, axis=-1, keepdims=True)
    )


def unit_rows(proj):
    factor = lax.rsqrt(jnp.sum(proj * proj, axis=-1, keepdims=True) + 1e-06)
    return (proj * factor, factor)


def matmul(left, right):
    return jnp.dot(left, right, preferred_element_type=F32)


def dot_nt(left, right):
    return lax.dot_general(left, right, (((1,), (1,)), ((), ())), preferred_element_type=F32)


def dot_tn(left, right):
    return lax.dot_general(left, right, (((0,), (0,)), ((), ())), preferred_element_type=F32)


def chunks(total, size):
    def wrap(body):
        @pl.loop(0, total // size)
        def step(j):
            body(pl.ds(pl.multiple_of(j * size, size), size))

    return wrap


def thirds(value):
    high = value.astype(BF16)
    rest = value - high.astype(F32)
    mid = rest.astype(BF16)
    return high, mid, (rest - mid.astype(F32)).astype(BF16)


def norm_rows(x, gain, shift):
    normed, rstd = normalize(x)
    return (normed * gain + shift).astype(BF16)


def head_masks(dtype, value):
    lane = lax.broadcasted_iota(jnp.int32, (1, 2 * HEAD), 1)
    first = jnp.where(lane < HEAD, value, 0.0).astype(dtype)
    second = jnp.where(lane < HEAD, 0.0, value).astype(dtype)
    return first, second


def both_heads(block, masks):
    return jnp.concatenate([block * masks[0], block * masks[1]], axis=0)


def merge_heads(stacked):
    half = stacked.shape[0] // 2
    lane = lax.broadcasted_iota(jnp.int32, (1, 2 * HEAD), 1)
    return jnp.where(lane < HEAD, stacked[:half], stacked[half:])


def softmax_unit(query, keys, mask, masks):
    scores = dot_nt(both_heads(query, masks), keys)
    scores = jnp.where(mask, scores, -1000000000.0)
    top = jnp.max(scores, axis=-1, keepdims=True)
    expo = jnp.exp(scores - top)
    return expo * (1.0 / jnp.sum(expo, axis=-1, keepdims=True))


def image_attention(x, gains, shifts, w_qkv, w_out, second, act, qkv, mixed):
    rows, width = x.shape
    group = GROUP_PAD

    @chunks(rows, group)
    def _(at):
        act[at, :] = norm_rows(x[at, :].astype(F32), gains[0:1, :], shifts[0:1, :])

    w_qkv = w_qkv()

    @chunks(3 * width, 256)
    def _(at):
        qkv[:, at] = matmul(act[...], w_qkv[:, at]).astype(BF16)

    masks = head_masks(BF16, 0.125)
    own = lax.broadcasted_iota(jnp.int32, (2 * group, group), 0)
    own = jnp.where(own >= group, own - group, own)
    other = lax.broadcasted_iota(jnp.int32, (2 * group, group), 1)
    mask = picture(own) == picture(other)

    @chunks(rows, group)
    def _(at):
        for start in range(0, width, 2 * HEAD):
            cols = slice(start, start + 2 * HEAD)
            keys = qkv[at, width + start : width + start + 2 * HEAD]
            values = qkv[at, 2 * width + start : 2 * width + start + 2 * HEAD]
            probs = softmax_unit(qkv[at, cols], keys, mask, masks)
            mixed[at, cols] = merge_heads(matmul(probs.astype(BF16), values)).astype(BF16)

    w_out = w_out()

    @chunks(width, 256)
    def _(at):
        second[:, at] = x[:, at].astype(F32) + matmul(mixed[...], w_out[:, at])


def picture(place):
    return jnp.where(place >= PATCHES, 1, 0) + jnp.where(place >= 2 * PATCHES, 1, 0)


def image_pool(value):
    value = value.reshape(-1, GROUP_PAD, value.shape[1])
    which = picture(lax.broadcasted_iota(jnp.int32, (1, GROUP_PAD, 1), 1))
    parts = [jnp.sum(jnp.where(which == kind, value, 0.0), axis=1) for kind in range(2)]
    return jnp.concatenate(parts, axis=0) * (1.0 / PATCHES)


def image_inner(second, gains, shifts, biases, w_in, pooled, pooled_second, act):
    rows, width = second.shape
    units = pooled.shape[1]

    @chunks(rows, GROUP_PAD)
    def _(at):
        act[at, :] = norm_rows(second[at, :], gains[1:2, :], shifts[1:2, :])

    for start in range(0, width, 256):
        pooled_second[:, start : start + 256] = image_pool(second[:, start : start + 256])
    w_in = w_in()

    @chunks(units, 256)
    def _(at):
        hidden = gelu(matmul(act[...], w_in[:, at]) + biases[:, at]).astype(BF16).astype(F32)
        pooled[:, at] = image_pool(hidden)


def image_embed(pooled, pooled_second, biases, w_down, w_proj, emb):
    images, units = pooled.shape
    high, mid, unused = thirds(pooled[...])
    w_down = w_down()
    y = matmul(jnp.concatenate([high, mid], axis=0), w_down[...])
    y = y[:images] + y[images:] + pooled_second[...] + biases[:, units:]
    emb[...] = unit_rows(matmul(y.astype(BF16), w_proj()[...]))[0].astype(BF16)


def text_attention(x, caption_col, caption_row, gains, shifts, w_qkv, w_out, qkv, probs, mixed, second, act):
    rows, width = x.shape
    group = 2 * HEAD
    act[...] = norm_rows(x[...].astype(F32), gains[0:1, :], shifts[0:1, :])
    w_qkv = w_qkv()

    @chunks(3 * width, 256)
    def _(at):
        qkv[:, at] = matmul(act[...], w_qkv[:, at]).astype(BF16)

    masks = head_masks(BF16, 0.125)
    unit = 0
    for top in range(0, rows, group):
        at = slice(top, top + group)
        same = caption_col[at, :] == caption_row[:, at]
        mask = jnp.concatenate([same, same], axis=0)
        for start in range(0, width, 2 * HEAD):
            cols = slice(start, start + 2 * HEAD)
            keys = qkv[at, width + start : width + start + 2 * HEAD]
            values = qkv[at, 2 * width + start : 2 * width + start + 2 * HEAD]
            prob = softmax_unit(qkv[at, cols], keys, mask, masks)
            probs[unit] = prob
            unit += 1
            mixed[at, cols] = merge_heads(matmul(prob.astype(BF16), values)).astype(BF16)

    w_out = w_out()

    @chunks(width, 256)
    def _(at):
        second[:, at] = x[:, at].astype(F32) + matmul(mixed[...], w_out[:, at])


def caption_member(caption_row, captions):
    index = lax.broadcasted_iota(jnp.int32, (captions, caption_row.shape[1]), 0)
    return (index == caption_row[...]).astype(F32)


def text_inner(second, caption_row, gains, shifts, biases, w_in, hidden, slope, hidden_sum, act):
    units = hidden.shape[1]
    act[...] = norm_rows(second[...], gains[1:2, :], shifts[1:2, :])
    low = caption_member(caption_row, hidden_sum.shape[0]).astype(BF16)
    w_in = w_in()

    @chunks(units, 256)
    def _(at):
        z = matmul(act[...], w_in[:, at]) + biases[:, at]
        inside = jnp.tanh(0.7978845608028654 * (z + 0.044715 * z * z * z))
        value = (0.5 * z * (1.0 + inside)).astype(BF16)
        hidden[:, at] = value
        slope[:, at] = 0.5 * (1.0 + inside) + 0.5 * z * (1.0 - inside * inside) * (
            0.7978845608028654 * (1.0 + 3.0 * 0.044715 * z * z)
        )
        hidden_sum[:, at] = matmul(low, value).astype(BF16)


def text_outer(second, hidden, caption_row, biases, w_down, out, pool_low):
    width = second.shape[1]
    units = hidden.shape[1]
    member = caption_member(caption_row, pool_low.shape[0])
    low = member.astype(BF16)
    count = jnp.sum(member, axis=1, keepdims=True)
    w_down = w_down()

    @chunks(width, 256)
    def _(at):
        outer = biases[:, pl.ds(pl.multiple_of(units + at.start, 256), 256)]
        y = second[:, at] + matmul(hidden[...], w_down[:, at]) + outer
        out[:, at] = y.astype(BF16)
        total = sum(matmul(low, part) for part in thirds(y))
        pool_low[:, at] = (total / count).astype(BF16)


def core_split(table, value, devices, mine, theirs):
    own = value.shape[0] // devices
    value = value.reshape(devices // 2, 2, own, value.shape[1])
    first = table[CORE] == 0
    even = value[:, 0].reshape(-1, value.shape[3])
    odd = value[:, 1].reshape(-1, value.shape[3])
    mine[...] = jnp.where(first, even, odd).astype(BF16)
    theirs[...] = jnp.where(first, odd, even).astype(BF16)


def back_inner(
    devices, table, each, caption_col, second, slope, gains, shifts, w_down, w_in, w_out,
    mine, theirs, d_second, d_mixed, sums_in, sums_out, act_t, act_u, both, d_act,
):
    rows, width = second.shape
    units = slope.shape[1]
    captions = each.shape[0]
    index = lax.broadcasted_iota(jnp.int32, (rows, 3 * captions), 1)
    index = jnp.where(index >= captions, index - captions, index)
    index = jnp.where(index >= captions, index - captions, index)
    member = (caption_col[...] == index).astype(BF16)
    normed, rstd = normalize(second[...])
    act = normed * gains[1:2, :] + shifts[1:2, :]
    core_split(table, act.T, devices, act_t, act_u)
    each_low = each[...].astype(BF16)
    w_down = w_down()

    @chunks(units, 256)
    def _(at):
        both[:, at] = jnp.concatenate(thirds(dot_nt(each_low, w_down[at, :])), axis=0)

    d_act[...] = jnp.zeros_like(d_act)
    w_in = w_in()

    @chunks(units, 256)
    def _(at):
        d_inner = matmul(member, both[:, at]) * slope[:, at]
        low = d_inner.astype(BF16)
        sums_in[:, at] = jnp.sum(low.astype(F32), axis=0, keepdims=True)
        theirs[:, at] = matmul(act_u[...], low).astype(BF16)
        mine[:, at] = matmul(act_t[...], low).astype(BF16)
        d_act[...] += dot_nt(low, w_in[:, at])

    d_y = matmul(member, jnp.concatenate(thirds(each[...]), axis=0))
    grad = d_act[...]
    sums_out[0:1, :] = jnp.sum(d_y, axis=0, keepdims=True)
    sums_out[1:2, :] = jnp.sum(grad * normed, axis=0, keepdims=True)
    sums_out[2:3, :] = jnp.sum(grad, axis=0, keepdims=True)
    d_two = d_y + norm_back(grad * gains[1:2, :], normed, rstd)
    d_second[...] = d_two
    low_two = d_two.astype(BF16)
    d_mixed[...] = dot_nt(low_two, w_out()[...]).astype(BF16)


def back_attention(
    devices, table, x, d_second, d_mixed, qkv, probs, mixed, gains, shifts, w_qkv,
    mine, theirs, text_grad, sums, d_qkv, act_t, act_u, mixed_t, mixed_u, d_act,
):
    rows, width = x.shape
    group = 2 * HEAD
    normed, rstd = normalize(x[...].astype(F32))
    act = normed * gains[0:1, :] + shifts[0:1, :]
    core_split(table, act.T, devices, act_t, act_u)
    core_split(table, mixed[...].astype(F32).T, devices, mixed_t, mixed_u)
    ones = head_masks(BF16, 1.0)
    masks = head_masks(BF16, 0.125)
    unit = 0
    for top in range(0, rows, group):
        at = slice(top, top + group)
        for start in range(0, width, 2 * HEAD):
            cols = slice(start, start + 2 * HEAD)
            key_cols = slice(width + start, width + start + 2 * HEAD)
            value_cols = slice(2 * width + start, 2 * width + start + 2 * HEAD)
            prob = probs[unit]
            unit += 1
            d_out = both_heads(d_mixed[at, cols], ones)
            query = both_heads(qkv[at, cols], masks)
            d_qkv[at, value_cols] = dot_tn(prob.astype(BF16), d_out).astype(BF16)
            d_prob = dot_nt(d_out, qkv[at, value_cols])
            d_score = (prob * (d_prob - jnp.sum(prob * d_prob, axis=-1, keepdims=True))).astype(BF16)
            d_qkv[at, cols] = (0.125 * merge_heads(matmul(d_score, qkv[at, key_cols]))).astype(BF16)
            d_qkv[at, key_cols] = dot_tn(d_score, query).astype(BF16)

    d_low = d_second[...].astype(BF16)
    for start in range(0, width, 256):
        at = slice(start, start + 256)
        to = slice(3 * width + start, 3 * width + start + 256)
        theirs[:, to] = matmul(mixed_u[...], d_low[:, at]).astype(BF16)
        mine[:, to] = matmul(mixed_t[...], d_low[:, at]).astype(BF16)
    d_act[...] = jnp.zeros_like(d_act)
    w_qkv = w_qkv()

    @chunks(3 * width, 256)
    def _(at):
        theirs[:, at] = matmul(act_u[...], d_qkv[:, at]).astype(BF16)
        mine[:, at] = matmul(act_t[...], d_qkv[:, at]).astype(BF16)
        d_act[...] += dot_nt(d_qkv[:, at], w_qkv[:, at])

    grad = d_act[...]
    sums[0:1, :] = jnp.sum(grad * normed, axis=0, keepdims=True)
    sums[1:2, :] = jnp.sum(grad, axis=0, keepdims=True)
    text_grad[...] = d_second[...] + norm_back(grad * gains[0:1, :], normed, rstd)


class Weight:
    def __init__(self, rows, cols):
        self.dims = (rows, cols)
        self.parts = []

    def add(self, array, lead, start, width, row, row_unit, col=None):
        self.parts.append((array, lead, start, width, row, row_unit, col))


def run(kernel, outs, scratch, table, operands, weights, us=5, passes_table=False):
    arrays = []
    for weight in weights:
        for part in weight.parts:
            if not any(part[0] is a for a in arrays):
                arrays.append(part[0])
    places = {id(a): i for i, a in enumerate(arrays)}
    n_op, n_arr, n_out, n_w = len(operands), len(arrays), len(outs), len(weights)

    def body(*refs):
        table_ref, refs = refs[0], refs[1:]
        ops, refs = refs[:n_op], refs[n_op:]
        arrs, refs = refs[:n_arr], refs[n_arr:]
        out, refs = refs[:n_out], refs[n_out:]
        held, refs = refs[:n_w], refs[n_w:]
        if n_w:
            sems, refs = refs[0], refs[1:]
        waits = []
        for i, weight in enumerate(weights):
            for array, lead, start, width, row, row_unit, col in weight.parts:
                at = 0 if row is None else pl.multiple_of(table_ref[row] * row_unit, 16)
                to = 0 if col is None else pl.multiple_of(table_ref[col] * width, 128)
                pltpu.make_async_copy(
                    arrs[places[id(array)]].at[lead, :, pl.ds(start, width)],
                    held[i].at[pl.ds(at, array.shape[1]), pl.ds(to, width)],
                    sems.at[i],
                ).start()

            def wait(i=i):
                pltpu.make_async_copy(held[i], held[i], sems.at[i]).wait()
                return held[i]

            waits.append(wait)
        if passes_table:
            ops = (table_ref, *ops)
        kernel(*ops, *waits, *out, *refs)

    vmem = pl.BlockSpec(memory_space=pltpu.VMEM)
    moved = sum(a.size * a.dtype.itemsize for a in (*operands, *outs))
    moved += sum(w.dims[0] * w.dims[1] * 2 for w in weights)
    held = sum(a.size * a.dtype.itemsize for a in (*operands, *outs))
    return pl.pallas_call(
        body,
        out_shape=outs,
        in_specs=[pl.BlockSpec(memory_space=pltpu.SMEM)] + [vmem] * n_op + [pl.BlockSpec(memory_space=pl.ANY)] * n_arr,
        out_specs=[vmem] * n_out,
        scratch_shapes=[pltpu.VMEM(w.dims, BF16) for w in weights]
        + ([pltpu.SemaphoreType.DMA((n_w,))] if n_w else [])
        + [pltpu.VMEM(*s) for s in scratch],
        compiler_params=pltpu.CompilerParams(vmem_limit_bytes=56 << 20),
        cost_estimate=pl.CostEstimate(flops=us * 1100000000, bytes_accessed=moved, transcendentals=0),
    )(table, *operands, *arrays)


def shape(dims, dtype):
    return jax.ShapeDtypeStruct(dims, dtype)


class Grid:
    def __init__(self, devices, sizes):
        self.devices = devices
        self.sizes = sizes
        strides = []
        step = devices
        for size in sizes:
            step //= size
            strides.append(step)
        self.strides = strides
        self.regular = len(sizes) == 4 and sizes[1:] == [2, 2, 2]

    def place(self):
        index = lax.axis_index("blk")
        return [(index // st) % size for size, st in zip(self.sizes, self.strides)]

    def shift(self, value, axis, step):
        size, stride = self.sizes[axis], self.strides[axis]
        pairs = []
        for i in range(self.devices):
            at = (i // stride) % size
            pairs.append((i, i + ((at + step) % size - at) * stride))
        return lax.ppermute(value, "blk", pairs)

    def table(self):
        place = self.place()
        chips = []
        for dz, dy, dx in self.offsets():
            origin = [(p - d) % s for p, d, s in zip(place, (dz, dy, dx), self.sizes)]
            chips.append(sum(o * st for o, st in zip(origin, self.strides)) // 2)
        chips = jnp.stack(chips)
        core = place[3]
        return jnp.concatenate([jnp.stack([core, 1 - core]), chips, 2 * chips + core, 2 * chips + 1 - core]).astype(
            jnp.int32
        )

    def offsets(self):
        z, y, x, unused = self.sizes
        return [(dz, dy, dx) for dz in range(z) for dy in range(y) for dx in range(x)]

    def row_of(self, offset, kind):
        chips = self.devices // 2
        return 2 + self.offsets().index(offset) + {"chip": 0, "own": chips, "other": 2 * chips}[kind]

    def line(self, value):
        return jnp.stack([value] + [self.shift(value, 0, k) for k in range(1, self.sizes[0])])

    def square(self, line):
        return self.shift(line, 2, 1), self.shift(line, 1, 1)

    def corner(self, by_x, by_y):
        half = self.sizes[0] // 2
        return self.shift(by_x[:half], 1, 1), self.shift(by_y[half:], 2, 1)

    def pieces(self, line, by_x, by_y, via_x, via_y):
        zs = range(self.sizes[0])
        half = self.sizes[0] // 2
        return [
            (line, [(z, 0, 0) for z in zs]),
            (by_x, [(z, 0, 1) for z in zs]),
            (by_y, [(z, 1, 0) for z in zs]),
            (via_x, [(z, 1, 1) for z in zs[:half]]),
            (via_y, [(z, 1, 1) for z in zs[half:]]),
        ]

    def pieces_z_last(self, squares):
        flat = [(0, 0), (0, 1), (1, 0), (1, 1)]
        return [(square, [(z, *f) for f in flat]) for z, square in enumerate(squares)]

    def across(self, pieces):
        return [(self.shift(array, 3, 1), offsets) for array, offsets in pieces]

    def reduce(self, mine, theirs):
        z, y, x, unused = self.place()
        depth = self.sizes[0]
        cols = mine.shape[1]

        def take(value, at, axis):
            return lax.dynamic_index_in_dim(value, at, axis, keepdims=False)

        def low(value):
            return value.astype(BF16)

        got = self.shift(theirs, 3, 1)
        total = (mine.astype(F32) + got.astype(F32)).reshape(depth, 2, 2, -1, cols)
        left, right = total[..., : cols // 2], total[..., cols // 2 :]
        left_got = self.shift(low(take(left, 1 - x, 2)), 2, 1)
        right_got = self.shift(low(take(right, 1 - y, 1)), 1, 1)
        left = take(left, x, 2) + left_got.astype(F32)
        right = take(right, y, 1) + right_got.astype(F32)
        left_got = self.shift(low(take(left, 1 - y, 1)), 1, 1)
        right_got = self.shift(low(take(right, 1 - x, 1)), 2, 1)
        left = take(left, y, 1) + left_got.astype(F32)
        right = take(right, x, 1) + right_got.astype(F32)
        line = jnp.concatenate([left, right], axis=-1)
        total = take(line, z, 0)
        for k in range(1, depth):
            total = total + self.shift(low(take(line, (z + k) % depth, 0)), 0, k).astype(F32)
        return total


def after(value, *earlier):
    return lax.optimization_barrier((value, *earlier))[0]


CORE = 0
OTHER = 1


def to_all(value, devices):
    return lax.all_to_all(jnp.broadcast_to(value[None], (devices, *value.shape)), "blk", 0, 0)


def pair_up(grid, weights):
    first = lax.axis_index("blk") % 2 == 0
    left = jnp.concatenate([w[:, : w.shape[1] // 2] for w in weights], axis=1)
    right = jnp.concatenate([w[:, w.shape[1] // 2 :] for w in weights], axis=1)
    keep = jnp.where(first, left, right)
    got = grid.shift(jnp.where(first, right, left), 3, 1)
    return jnp.concatenate([jnp.where(first, keep, got), jnp.where(first, got, keep)], axis=0)


def halves(grid, weight, pieces, others, start):
    for group, col in ((pieces, CORE), (others, OTHER)):
        for array, offsets in group:
            for lead, offset in enumerate(offsets):
                row = grid.row_of(offset, "chip")
                weight.add(array, lead, start, weight.dims[1] // 2, row, array.shape[1], col)
    return weight


def rows_of(grid, weight, pieces, others):
    for group, kind in ((pieces, "own"), (others, "other")):
        for array, offsets in group:
            for lead, offset in enumerate(offsets):
                weight.add(array, lead, 0, weight.dims[1], grid.row_of(offset, kind), array.shape[1])
    return weight


def gathered(part):
    full = lax.all_gather(part, "blk", axis=0, tiled=True)
    weight = Weight(*full.shape)
    weight.add(full[None], 0, 0, full.shape[1], None, 0)
    return weight


def reduce_grads(grid, mine, theirs, width):
    own = width // grid.devices
    if grid.regular and own % 8 == 0:
        return grid.reduce(mine, theirs)
    both = jnp.where(lax.axis_index("blk") % 2 == 0, jnp.stack([mine, theirs], 0), jnp.stack([theirs, mine], 0))
    both = both.reshape(2, grid.devices // 2, own, -1).transpose(1, 0, 2, 3).reshape(width, -1)
    return lax.psum_scatter(both, "blk", scatter_dimension=0, tiled=True).astype(F32)


def head_tile(proj, factor, image_emb, scale, row_lse, col_lse, pairs, sim):
    hit = pairs[:, None] == jnp.arange(image_emb.shape[0], dtype=jnp.int32)[None, :]
    weights_sim = (
        0.5 * jnp.exp(sim - row_lse[:, None]) + 0.5 * jnp.exp(sim - col_lse[None, :]) - hit.astype(F32)
    )
    d_emb = scale * matmul(weights_sim.astype(BF16), image_emb)
    d_proj = factor * d_emb - proj * (factor * factor * factor) * jnp.sum(d_emb * proj, axis=-1, keepdims=True)
    pos = jnp.sum(jnp.where(hit, sim, 0.0), axis=1)
    pair_col = jnp.sum(jnp.where(hit, col_lse[None, :], 0.0), axis=1)
    return (d_proj.astype(BF16), 0.5 * (row_lse - pos) + 0.5 * (pair_col - pos))


def on_device(grid, *args):
    (
        text_tokens,
        segment_ids,
        pair_index,
        image_tokens,
        logit_scale,
        img_gains,
        img_shifts,
        img_qkv,
        img_out,
        img_in,
        img_down,
        img_biases,
        img_proj,
        txt_gains,
        txt_shifts,
        txt_qkv,
        txt_out,
        txt_in,
        txt_down,
        txt_biases,
        txt_proj,
    ) = args
    devices = grid.devices
    width = text_tokens.shape[1]
    units = img_in.shape[1]
    scale = logit_scale[0]
    rows, length = segment_ids.shape
    tokens = rows * length
    captions = pair_index.shape[0]
    images = image_tokens.shape[0] // PATCHES
    device = lax.axis_index("blk")
    own = width // devices
    table = grid.table()

    caption_of = (jnp.arange(rows, dtype=jnp.int32)[:, None] * CAPS + segment_ids).reshape(tokens)
    caption_col, caption_row = caption_of[:, None], caption_of[None, :]
    member = (jnp.arange(captions, dtype=jnp.int32)[:, None] == caption_row).astype(F32)
    counts = jnp.sum(member, axis=1)

    vec = (img_gains.shape[0], img_shifts.shape[0], img_biases.shape[0])
    vectors = jnp.concatenate(
        [
            img_gains,
            img_shifts,
            img_biases,
            txt_gains,
            txt_shifts,
            txt_biases,
            (pair_index // 64).astype(BF16),
            (pair_index % 64).astype(BF16),
            counts.astype(BF16),
        ]
    )
    vectors = to_all(vectors, devices).reshape(devices, -1).astype(F32)
    parts = []
    start = 0
    for size in vec + vec + (captions,) * 3:
        parts.append(vectors[:, start : start + size].reshape(-1))
        start += size
    img_g, img_s = parts[0].reshape(2, width), parts[1].reshape(2, width)
    gains, shifts = parts[3].reshape(2, width), parts[4].reshape(2, width)
    img_b, biases = parts[2].reshape(1, -1), parts[5].reshape(1, -1)
    every_pair = parts[6].astype(jnp.int32) * 64 + parts[7].astype(jnp.int32)
    every_count = parts[8]

    regular = grid.regular and own % 8 == 0
    if regular:
        tdx, tdy = grid.square(txt_down)
        idl = grid.line(img_down)
        idl = after(idl, tdx, tdy)
        td_square = jnp.stack([txt_down, tdx, tdy, grid.shift(tdx, 1, 1)])
        pair = pair_up(grid, [txt_qkv, txt_out, img_qkv, img_out, img_in, img_proj, txt_in, txt_proj])
        cuts = [0, 4 * width, 4 * width + (units + width) // 2, 4 * width + units + width]
        idx, idy = grid.square(idl)
        idv = grid.corner(idx, idy)
        line1 = grid.line(pair[:, : cuts[1]])
        line1 = after(line1, idx, idy, td_square)
        x1, y1 = grid.square(line1)
        line2 = after(grid.line(after(pair[:, cuts[1] : cuts[2]], idx, idy)), x1, y1, *idv)
        line3 = grid.line(after(pair[:, cuts[2] :], line1))
        ring1 = grid.shift(after(td_square, line1), 0, 1)
        v1 = grid.corner(x1, y1)
        x2, y2 = grid.square(line2)
        one = grid.pieces(line1, x1, y1, *v1)
        one_x = grid.across(one)
        text_w = [
            halves(grid, Weight(width, 3 * width), one, one_x, 0),
            halves(grid, Weight(width, width), one, one_x, 3 * width // 2),
        ]
        image_w = [
            halves(grid, Weight(width, 3 * width), one, one_x, 2 * width),
            halves(grid, Weight(width, width), one, one_x, 2 * width + 3 * width // 2),
        ]
        table1 = after(table, line2, line3)
    else:
        image_w = [gathered(w) for w in (img_qkv, img_out, img_in, img_proj, img_down)]
        text_w = [gathered(w) for w in (txt_qkv, txt_out, txt_in, txt_proj, txt_down)]
        table1 = table

    heads = tokens // (2 * HEAD) * (width // (2 * HEAD))
    qkv, probs, mixed, second = run(
        text_attention,
        [
            shape((tokens, 3 * width), BF16),
            shape((heads, 4 * HEAD, 2 * HEAD), F32),
            shape((tokens, width), BF16),
            shape((tokens, width), F32),
        ],
        [((tokens, width), BF16)],
        table1,
        [text_tokens, caption_col, caption_row, gains, shifts],
        text_w[:2],
        us=10,
    )
    table2 = table
    if regular:
        x2k, y2k, unused = lax.optimization_barrier((x2, y2, second))
        v2 = grid.corner(x2k, y2k)
        x3, y3 = grid.square(after(line3, x2k))
        ring2 = grid.shift(ring1, 0, 1)
        table2 = after(table, x2k, y2k, ring1)
    pairs = images // 2
    padded = pairs * GROUP_PAD
    x_image = jnp.pad(
        image_tokens.reshape(pairs, 2 * PATCHES, width), ((0, 0), (0, GROUP_PAD - 2 * PATCHES), (0, 0))
    ).reshape(padded, width)
    image_second = run(
        image_attention,
        [shape((padded, width), F32)],
        [((padded, width), BF16), ((padded, 3 * width), BF16), ((padded, width), BF16)],
        table2,
        [x_image, img_g, img_s],
        image_w[:2],
        us=19,
    )[0]
    table3 = table
    if regular:
        x3, y3, unused = lax.optimization_barrier((x3, y3, image_second))
        v3 = grid.corner(x3, y3)
        ring3 = grid.shift(ring2, 0, 1)
        table3 = after(table, x3, y3, ring2)
        two = grid.pieces(line2, x2, y2, *v2)
        two_x = grid.across(two)
        three = grid.pieces(line3, x3, y3, *v3)
        three_x = grid.across(three)
        img_d = grid.pieces(idl, idx, idy, *idv)
        txt_d = grid.pieces_z_last([td_square, ring1, ring2, ring3])
        image_w += [
            halves(grid, Weight(width, units), two, two_x, 0),
            halves(grid, Weight(width, width), two, two_x, units // 2),
            rows_of(grid, Weight(units, width), img_d, grid.across(img_d)),
        ]
        text_w += [
            halves(grid, Weight(width, units), three, three_x, 0),
            halves(grid, Weight(width, width), three, three_x, units // 2),
            rows_of(grid, Weight(units, width), txt_d, grid.across(txt_d)),
        ]
    pooled, pooled_second = run(
        image_inner,
        [shape((images, units), F32), shape((images, width), F32)],
        [((padded, width), BF16)],
        table3,
        [image_second, img_g, img_s, img_b],
        image_w[2:3],
        us=13,
    )
    hidden, slope, hidden_sum = run(
        text_inner,
        [shape((tokens, units), BF16), shape((tokens, units), F32), shape((captions, units), BF16)],
        [((tokens, width), BF16)],
        table,
        [second, caption_row, gains, shifts, biases],
        text_w[2:3],
        us=7,
    )
    image_emb = run(
        image_embed,
        [shape((images, width), BF16)],
        [],
        table,
        [pooled, pooled_second, img_b],
        [image_w[4], image_w[3]],
        us=5,
    )[0]
    image_emb = image_emb.reshape(2, pairs, width).transpose(1, 0, 2).reshape(images, width)
    image_emb = to_all(image_emb, devices).reshape(-1, width)
    hidden_sum = lax.all_to_all(hidden_sum, "blk", split_axis=1, concat_axis=0, tiled=True)
    text_out, pool_low = run(
        text_outer,
        [shape((tokens, width), BF16), shape((captions, width), BF16)],
        [],
        table,
        [second, hidden, caption_row, biases],
        text_w[4:5],
        us=5,
    )
    w_proj = run(copy_weight, [shape((width, width), BF16)], [], table, [], text_w[3:4])[0]

    pool_all = to_all(pool_low, devices).reshape(-1, width)
    total = pool_all.shape[0]
    col_max = jnp.full((total,), -1e30, F32)
    col_sum = jnp.zeros((total,), F32)
    held = []
    for start in range(0, total, TILE):
        proj = matmul(pool_all[start : start + TILE], w_proj)
        unit, factor = unit_rows(proj)
        sim = scale * dot_nt(unit.astype(BF16), image_emb)
        top = jnp.max(sim, axis=1)
        row_lse = top + jnp.log(jnp.sum(jnp.exp(sim - top[:, None]), axis=1))
        new_max = jnp.maximum(col_max, jnp.max(sim, axis=0))
        col_sum = col_sum * jnp.exp(col_max - new_max) + jnp.sum(jnp.exp(sim - new_max[None, :]), axis=0)
        col_max = new_max
        held.append((proj, factor, row_lse, sim))
    col_lse = col_max + jnp.log(col_sum)
    d_proj = []
    losses = []
    for start, (proj, factor, row_lse, sim) in zip(range(0, total, TILE), held):
        grad, loss = head_tile(
            proj, factor, image_emb, scale, row_lse, col_lse, every_pair[start : start + TILE], sim
        )
        d_proj.append(grad)
        losses.append(loss)
    d_proj = jnp.concatenate(d_proj)
    pair_loss = lax.dynamic_slice_in_dim(jnp.concatenate(losses), device * captions, captions)
    grad_proj = dot_tn(lax.dynamic_slice_in_dim(pool_all, device * own, own, axis=1), d_proj)
    d_each = dot_nt(d_proj, w_proj) / every_count[:, None]
    grad_down = dot_tn(hidden_sum, d_each.astype(BF16))
    d_mine = lax.dynamic_slice_in_dim(d_each, device * captions, captions)

    half = width // 2
    mine_in, theirs_in, d_second, d_mixed, sums_in, sums_out = run(
        functools.partial(back_inner, devices),
        [
            shape((half, units), BF16),
            shape((half, units), BF16),
            shape((tokens, width), F32),
            shape((tokens, width), BF16),
            shape((1, units), F32),
            shape((8, width), F32),
        ],
        [
            ((half, tokens), BF16),
            ((half, tokens), BF16),
            ((3 * captions, units), BF16),
            ((tokens, width), F32),
        ],
        table,
        [d_mine, caption_col, second, slope, gains, shifts],
        [text_w[4], text_w[2], text_w[1]],
        us=18,
        passes_table=True,
    )
    mine_qkv, theirs_qkv, text_grad, sums_qkv = run(
        functools.partial(back_attention, devices),
        [
            shape((half, 4 * width), BF16),
            shape((half, 4 * width), BF16),
            shape((tokens, width), F32),
            shape((8, width), F32),
        ],
        [((tokens, 3 * width), BF16)] + [((half, tokens), BF16)] * 4 + [((tokens, width), F32)],
        table,
        [text_tokens, d_second, d_mixed, qkv, probs, mixed, gains, shifts],
        text_w[:1],
        us=14,
        passes_table=True,
    )
    grad_in = reduce_grads(grid, mine_in, theirs_in, width)
    grad_qkv = reduce_grads(grid, mine_qkv, theirs_qkv, width)
    sums = jnp.concatenate(
        [
            jnp.concatenate([sums_qkv[0], sums_out[1]]).reshape(devices, -1),
            jnp.concatenate([sums_qkv[1], sums_out[2]]).reshape(devices, -1),
            jnp.concatenate([sums_in[0], sums_out[0]]).reshape(devices, -1),
        ],
        axis=1,
    )
    sums = jnp.sum(lax.all_to_all(sums, "blk", 0, 0, tiled=True), axis=0)
    return (
        pair_loss,
        text_out,
        text_grad,
        sums[: vec[0]],
        sums[vec[0] : vec[0] + vec[1]],
        grad_qkv[:, : 3 * width],
        grad_qkv[:, 3 * width :],
        grad_in,
        grad_down,
        sums[vec[0] + vec[1] :],
        grad_proj,
    )


def copy_weight(weight, out):
    out[...] = weight()[...]


def axis_sizes(mesh):
    devices = list(mesh.devices.flat)
    places = [(*d.coords, d.core_on_chip) for d in devices]
    sizes = []
    stride = len(devices)
    left = [0, 1, 2, 3]
    while stride > 1 and left:
        for axis in left:
            size = 1 + max(p[axis] for p in places) - min(p[axis] for p in places)
            step = stride // size
            if size > 1 and all(
                p[axis] - places[0][axis] == (i // step) % size for i, p in enumerate(places)
            ):
                sizes.append(size)
                left.remove(axis)
                stride = step
                break
        else:
            return [len(devices)]
    return sizes


def solution(mesh):
    grid = Grid(mesh.shape["blk"], axis_sizes(mesh))
    row = P("blk", None)
    flat = P("blk")
    tower = (flat, flat, row, row, row, row, flat, row)

    def body(*args):
        return on_device(grid, *args)

    return jax.shard_map(
        body,
        mesh=mesh,
        in_specs=(row, row, flat, row, P()) + tower + tower,
        out_specs=(flat, row, row, flat, flat, row, row, row, row, flat, row),
        check_vma=False,
    )
```

time: 660 us -> 398 us (0.60); the launches traced: 647 us -> 397 us
  waiting for transfers between devices: 374 us -> 136 us
  Pallas kernels: 0 us -> 102 us
  starting transfers between devices: 3.95 us -> 96.9 us
  matrix products: 101 us -> 8.98 us
  local copies, waits for them, and re-layouts: 121 us -> 36.8 us
  other arithmetic: 32.1 us -> 12 us
  between operations: 15.6 us -> 3.32 us
    all_gather x3 -> x0, waiting for transfers between devices: 258 us -> none  [gather(): return lax.all_gather(part, 'blk', axis=0, tiled=True)]
    unnamed x5 -> x0, waiting for transfers between devices: 112 us -> none
    ppermute x0 -> x75, waiting for transfers between devices: none -> 110 us  [shift(): return lax.ppermute(value, 'blk', pairs)]
    pallas_call x0 -> x9, Pallas kernels: none -> 102 us  [run(): pl.pallas_call(body, out_shape=outs, in_specs=[pl.BlockSpec(memory_space=...]
    ppermute x0 -> x75, starting transfers between devices: none -> 76.8 us  [shift(): return lax.ppermute(value, 'blk', pairs)]
    dot_general x23 -> x4, matrix products: 56.6 us -> 5.89 us  [the longest x2 4.31 us: dot_tn(): lax.dot_general(left, right, (((0,), (0,)), ((), ())), preferred_element_...]
    reshape x21 -> x3, local copies, waits for them, and re-layouts: 46.7 us -> 1.1 us  [the longest x1 0.76 us: on_device(): image_emb.reshape(2, pairs, width).transpose(1, 0, 2).reshape(images, width)]
    dot_general x11 -> x2, matrix products: 44.2 us -> 3.09 us  [matmul(): return jnp.dot(left, right, preferred_element_type=F32)]
  transfers between devices with their start and end apart: 5 -> 80, of which waited for: 5 -> 23; matrix products, arithmetic and copies ran while one was open for 4% -> 10% of each run, Pallas kernels for 0% -> 18%
where the time goes in v2:
time: 398 us; the launch traced here: 397 us
  waiting for transfers between devices  136 us (34%)
  Pallas kernels  102 us (26%)
  starting transfers between devices  96.9 us (24%)
  local copies, waits for them, and re-layouts  36.8 us (9%)
  other arithmetic  12 us (3%)
  matrix products  8.98 us (2%)
    ppermute x75, waiting for transfers between devices, shift(): return lax.ppermute(value, 'blk', pairs)  110 us
    pallas_call x9, Pallas kernels, run(): pl.pallas_call(body, out_shape=outs, in_specs=[pl.BlockSpec(memory_space=...  102 us
    ppermute x75, starting transfers between devices, shift(): return lax.ppermute(value, 'blk', pairs)  76.8 us
    all_to_all x3, waiting for transfers between devices, to_all(): lax.all_to_all(jnp.broadcast_to(value[None], (devices, *value.shape)), 'b...  18.6 us
    all_to_all x3, starting transfers between devices, to_all(): lax.all_to_all(jnp.broadcast_to(value[None], (devices, *value.shape)), 'b...  13.6 us
    unnamed x112, local copies, waits for them, and re-layouts  10.8 us
  transfers between devices with their start and end apart: 80, of which 23 were waited for; matrix products, arithmetic and copies ran while one was open for 10% of the time, Pallas kernels for 18%

profile of v2, /device:TPU:0, one launch (start us, length us, event | category | flops | bytes accessed | tf_op | source)
XLA Modules:
  0.0 396.5 jit_solution(14277097819891928274)
XLA Ops:
  7.9 2.6 collective-permute-start.4
  12.0 1.6 collective-permute-start.1
  13.6 2.2 collective-permute-start.3
  15.8 1.9 collective-permute-start.2
  20.5 3.0 collective-permute-start.13
  23.5 12.6 %collective-permute-start.12 = (bf16[48,3072]{1,0:T(8,128)(2,1)S(1)}, bf16[48,3072]{1,0:T(8,128)(2,1)S(1)}, u32[]{:S(2)}, u32[]{:S(2)}) collective-permute-start(bf16[48,3072]{1,0:T(8,128)(2,1)S(1)} %pad_maximum_fusion.5), channel_id=1, source_target_pairs={{0,16},{1,17},{2,18},{3,19},{4,20},{5,21},{6,22},{7,23},{8,24},{9,... | collective-permute-start | bytes 884744 | tf_op jit(solution)/shard_map/ppermute | solution.py:441
  36.1 2.0 collective-permute-start.11
  40.2 14.1 %collective-permute-done.12 = bf16[48,3072]{1,0:T(8,128)(2,1)S(1)} collective-permute-done((bf16[48,3072]{1,0:T(8,128)(2,1)S(1)}, bf16[48,3072]{1,0:T(8,128)(2,1)S(1)}, u32[]{:S(2)}, u32[]{:S(2)}) %collective-permute-start.12) | collective-permute-done | bytes 294944 | tf_op jit(solution)/shard_map/ppermute | solution.py:441
  55.6 2.3 collective-permute-start.10
  58.2 1.9 collective-permute-start.8
  60.2 18.3 %collective-permute-done.16.refs_8_.refs_6_.refs_27_.refs_11_ = bf16[4,48,3072]{2,1,0:T(8,128)(2,1)S(1)} collective-permute-done((bf16[4,48,3072]{2,1,0:T(8,128)(2,1)S(1)}, bf16[4,48,3072]{2,1,0:T(8,128)(2,1)S(1)}, u32[]{:S(2)}, u32[]{:S(2)}) %collective-permute-start.16) | collective-permute-done | bytes 1179680 | tf_op jit(solution)/shard_map/ppermute | solution.py:441
  78.5 4.1 %collective-permute-start.21 = (bf16[48,1920]{1,0:T(8,128)(2,1)S(1)}, bf16[48,1920]{1,0:T(8,128)(2,1)S(1)}, u32[]{:S(2)}, u32[]{:S(2)}) collective-permute-start(bf16[48,1920]{1,0:T(8,128)(2,1)S(1)} %get-tuple-element.50), channel_id=1, source_target_pairs={{0,24},{1,25},{2,26},{3,27},{4,28},{5,29},{6,30},{7,31},{8,0},{9,1... | collective-permute-start | bytes 552968 | tf_op jit(solution)/shard_map/ppermute | solution.py:441
  88.4 9.3 %collective-permute-done.20 = bf16[48,1920]{1,0:T(8,128)(2,1)S(1)} collective-permute-done((bf16[48,1920]{1,0:T(8,128)(2,1)S(1)}, bf16[48,1920]{1,0:T(8,128)(2,1)S(1)}, u32[]{:S(2)}, u32[]{:S(2)}) %collective-permute-start.20) | collective-permute-done | bytes 184352 | tf_op jit(solution)/shard_map/ppermute | solution.py:441
  101.8 2.6 all-to-all-start
  107.2 4.4 %all-to-all-done = bf16[32,2,240]{2,1,0:T(2,128)(2,1)S(1)} async-done(((bf16[32,2,240]{2,1,0:T(2,128)(2,1)}), bf16[32,2,240]{2,1,0:T(2,128)(2,1)S(1)}, u32[]{:S(2)}, u32[]{:S(2)}) %all-to-all-start) | async-done | bytes 30752 | tf_op jit(solution)/shard_map/all_to_all | solution.py:529
  117.2 9.6 %shard_map.284 = (bf16[256,2304]{1,0:T(8,128)(2,1)}, f32[12,256,128]{2,1,0:T(8,128)}, bf16[256,768]{1,0:T(8,128)(2,1)}, f32[256,768]{1,0:T(8,128)}) custom-call(s32[50]{0:T(128)} %concatenate.44.refs_0_, bf16[256,768]{1,0:T(8,128)(2,1)} %refs_1_.3, s32[256,1]{1,0:T(8,128)} %broadcast_in_dim_reshape.10.refs_2_, ...), custom_call_target="tpu_custom_call" | custom-call | flops 11000000512 | bytes 9058304 | tf_op jit(solution)/shard_map/pallas_call | solution.py:402
  126.8 7.4 %collective-permute-done.30.refs_7_.refs_16_ = bf16[4,48,1920]{2,1,0:T(8,128)(2,1)S(1)} collective-permute-done((bf16[4,48,1920]{2,1,0:T(8,128)(2,1)S(1)}, bf16[4,48,1920]{2,1,0:T(8,128)(2,1)S(1)}, u32[]{:S(2)}, u32[]{:S(2)}) %collective-permute-start.30) | collective-permute-done | bytes 737312 | tf_op jit(solution)/shard_map/ppermute | solution.py:441
  140.5 11.5 %collective-permute-done.41.refs_7_.refs_9_ = bf16[4,96,768]{2,1,0:T(8,128)(2,1)} collective-permute-done((bf16[4,96,768]{2,1,0:T(8,128)(2,1)}, bf16[4,96,768]{2,1,0:T(8,128)(2,1)}, u32[]{:S(2)}, u32[]{:S(2)}) %collective-permute-start.41) | collective-permute-done | bytes 589856 | tf_op jit(solution)/shard_map/ppermute | solution.py:441
  153.4 19.1 %shard_map.285.refs_1_ = f32[896,768]{1,0:T(8,128)} custom-call(s32[50]{0:T(128)} %concatenate.44.refs_0_, bf16[896,768]{1,0:T(8,128)(2,1)} %bitcast.137, f32[2,768]{1,0:T(2,128)} %reshape_reshape.21.refs_2_, f32[2,768]{1,0:T(2,128)} %reshape_reshape.22.refs_3_, bf16[4,48,3072]{2,1,0:T(8,128)(2,1)} %copy-done.4, bf16[4,48,3072]{2,1,0:T(8,128)(2,1)} %copy-done.13, ...), custom_call_target="tpu_custom_call" | custom-call | flops 20899999744 | bytes 8859648 | tf_op jit(solution)/shard_map/pallas_call | solution.py:402
  176.6 8.0 %collective-permute-done.35.refs_10_.refs_5_.refs_19_ = bf16[2,48,1920]{2,1,0:T(8,128)(2,1)S(1)} collective-permute-done((bf16[2,48,1920]{2,1,0:T(8,128)(2,1)S(1)}, bf16[2,48,1920]{2,1,0:T(8,128)(2,1)S(1)}, u32[]{:S(2)}, u32[]{:S(2)}) %collective-permute-start.35) | collective-permute-done | bytes 368672 | tf_op jit(solution)/shard_map/ppermute | solution.py:441
  192.3 12.2 %shard_map.286 = (bf16[256,3072]{1,0:T(8,128)(2,1)}, f32[256,3072]{1,0:T(8,128)}, bf16[16,3072]{1,0:T(8,128)(2,1)}) custom-call(s32[50]{0:T(128)} %concatenate.44.refs_0_, f32[256,768]{1,0:T(8,128)} %get-tuple-element.52.refs_1_.refs_3_, s32[1,256]{1,0:T(1,128)} %broadcast_in_dim_reshape.9.refs_3_.refs_2_, ...), custom_call_target="tpu_custom_call" | custom-call | flops 7699999744 | bytes 10350592 | tf_op jit(solution)/shard_map/pallas_call | solution.py:402
  205.0 7.1 %shard_map.287 = (bf16[256,768]{1,0:T(8,128)(2,1)}, bf16[16,768]{1,0:T(8,128)(2,1)}) custom-call(s32[50]{0:T(128)} %concatenate.44.refs_0_, f32[256,768]{1,0:T(8,128)} %get-tuple-element.52.refs_1_.refs_3_, bf16[256,3072]{1,0:T(8,128)(2,1)} %get-tuple-element.60.refs_2_, s32[1,256]{1,0:T(1,128)} %broadcast_in_dim_reshape.9.refs_3_.refs_2_, ...), custom_call_target="tpu_custom_call" | custom-call | flops 5500000256 | bytes 7512064 | tf_op jit(solution)/shard_map/pallas_call | solution.py:402
  212.2 1.8 broadcast_in_dim.22
  213.9 5.1 %all-to-all-start.1 = ((bf16[32,16,768]{2,1,0:T(8,128)(2,1)}), bf16[32,16,768]{2,1,0:T(8,128)(2,1)S(1)}, u32[]{:S(2)}, u32[]{:S(2)}) async-start(bf16[32,16,768]{2,1,0:T(8,128)(2,1)} %broadcast_in_dim.22), calls=%async_computation.1 | async-start | bytes 1572864 | tf_op jit(solution)/shard_map/all_to_all | solution.py:529
  220.7 13.7 %shard_map.289 = (f32[16,3072]{1,0:T(8,128)}, f32[16,768]{1,0:T(8,128)}) custom-call(s32[50]{0:T(128)} %concatenate.44.refs_0_, f32[896,768]{1,0:T(8,128)} %shard_map.285.refs_1_, f32[2,768]{1,0:T(2,128)} %reshape_reshape.21.refs_2_, f32[2,768]{1,0:T(2,128)} %reshape_reshape.22.refs_3_, f32[1,3840]{1,0:T(1,128)} %reshape_reshape.23.refs_4_.refs_3_, ...), custom_call_target="tpu_custom_call" | custom-call | flops 14300000256 | bytes 7744512 | tf_op jit(solution)/shard_map/pallas_call | solution.py:402
  235.8 5.5 %shard_map.290 = bf16[16,768]{1,0:T(8,128)(2,1)} custom-call(s32[50]{0:T(128)} %concatenate.44.refs_0_, f32[16,3072]{1,0:T(8,128)} %get-tuple-element.63.refs_1_, f32[16,768]{1,0:T(8,128)} %get-tuple-element.64.refs_2_, f32[1,3840]{1,0:T(1,128)} %reshape_reshape.23.refs_4_.refs_3_, bf16[4,96,768]{2,1,0:T(8,128)(2,1)} %copy-done.10, ...), custom_call_target="tpu_custom_call" | custom-call | flops 5500000256 | bytes 6183936 | tf_op jit(solution)/shard_map/pallas_call | solution.py:402
  243.1 6.0 %all-to-all-start.2 = ((bf16[32,16,768]{2,1,0:T(8,128)(2,1)}), bf16[32,16,768]{2,1,0:T(8,128)(2,1)S(1)}, u32[]{:S(2)}, u32[]{:S(2)}) async-start(bf16[32,16,768]{2,1,0:T(8,128)(2,1)} %broadcast_in_dim.25), calls=%async_computation.2 | async-start | bytes 1572864 | tf_op jit(solution)/shard_map/all_to_all | solution.py:529
  250.1 3.1 shard_map.288
  253.1 2.1 multiply_reduce_fusion.1
  255.3 14.2 %all-to-all-done.2 = bf16[32,16,768]{2,1,0:T(8,128)(2,1)S(1)} async-done(((bf16[32,16,768]{2,1,0:T(8,128)(2,1)}), bf16[32,16,768]{2,1,0:T(8,128)(2,1)S(1)}, u32[]{:S(2)}, u32[]{:S(2)}) %all-to-all-start.2) | async-done | bytes 786464 | tf_op jit(solution)/shard_map/all_to_all | solution.py:529
  275.9 17.8 %shard_map.291 = (bf16[384,3072]{1,0:T(8,128)(2,1)}, bf16[384,3072]{1,0:T(8,128)(2,1)}, f32[256,768]{1,0:T(8,128)}, bf16[256,768]{1,0:T(8,128)(2,1)}, f32[1,3072]{1,0:T(1,128)}, /*index=5*/f32[8,768]{1,0:T(8,128)}) custom-call(s32[50]{0:T(128)} %concatenate.44.refs_0_, f32[16,768]{1,0:T(8,128)} %constant_dynamic-slice_fusion.8.refs_1_, ...), custom_call_target="tpu_custom_call" | custom-call | flops 19800000512 | bytes 20546560 | tf_op jit(solution)/shard_map/pallas_call | solution.py:402
  293.8 14.3 %shard_map.292 = (bf16[384,3072]{1,0:T(8,128)(2,1)}, bf16[384,3072]{1,0:T(8,128)(2,1)}, f32[256,768]{1,0:T(8,128)}, f32[8,768]{1,0:T(8,128)}) custom-call(s32[50]{0:T(128)} %concatenate.44.refs_0_, bf16[256,768]{1,0:T(8,128)(2,1)} %refs_1_.3, f32[256,768]{1,0:T(8,128)} %get-tuple-element.67.refs_2_, bf16[256,768]{1,0:T(8,128)(2,1)} %get-tuple-element.68.refs_3_, ...), custom_call_target="tpu_custom_call" | custom-call | flops 15399999488 | bytes 13799424 | tf_op jit(solution)/shard_map/pallas_call | solution.py:402
  309.1 3.7 all-to-all-start.4
  315.9 5.1 %all-to-all-done.4 = bf16[16,32,96]{2,0,1:T(8,128)(2,1)S(1)} async-done(((bf16[16,32,96]{2,0,1:T(8,128)(2,1)}), bf16[16,32,96]{2,0,1:T(8,128)(2,1)S(1)}, u32[]{:S(2)}, u32[]{:S(2)}) %all-to-all-start.4) | async-done | bytes 98336 | tf_op jit(solution)/shard_map/all_to_all | solution.py:774
  321.0 2.8 all-to-all-start.3
  323.8 2.4 fusion.4
  326.2 1.9 fusion.47
  328.7 2.1 all-to-all-done.3
  332.0 2.5 convert_add_fusion.1
  336.7 2.5 convert_add_fusion
  341.1 1.5 collective-permute-start.70
  342.6 8.7 %collective-permute-done.60 = bf16[4,2,24,1536]{3,2,0,1:T(8,128)(2,1)S(1)} collective-permute-done((bf16[4,2,24,1536]{3,2,0,1:T(8,128)(2,1)S(1)}, bf16[4,2,24,1536]{3,2,0,1:T(8,128)(2,1)S(1)}, u32[]{:S(2)}, u32[]{:S(2)}) %collective-permute-start.60) | collective-permute-done | bytes 589856 | tf_op jit(solution)/shard_map/ppermute | solution.py:441
  353.8 10.2 %collective-permute-done.68 = bf16[4,2,24,1536]{3,2,0,1:T(8,128)(2,1)S(1)} collective-permute-done((bf16[4,2,24,1536]{3,2,0,1:T(8,128)(2,1)S(1)}, bf16[4,2,24,1536]{3,2,0,1:T(8,128)(2,1)S(1)}, u32[]{:S(2)}, u32[]{:S(2)}) %collective-permute-start.68) | collective-permute-done | bytes 589856 | tf_op jit(solution)/shard_map/ppermute | solution.py:441
  366.4 4.5 %collective-permute-done.61 = bf16[4,24,1536]{2,1,0:T(8,128)(2,1)S(1)} collective-permute-done((bf16[4,24,1536]{2,1,0:T(8,128)(2,1)S(1)}, bf16[4,24,1536]{2,1,0:T(8,128)(2,1)S(1)}, u32[]{:S(2)}, u32[]{:S(2)}) %collective-permute-start.61) | collective-permute-done | bytes 294944 | tf_op jit(solution)/shard_map/ppermute | solution.py:441
  371.8 2.2 collective-permute-start.65
  377.0 2.2 collective-permute-start.73
  381.3 5.2 %collective-permute-done.65 = bf16[24,3072]{1,0:T(8,128)(2,1)S(1)} collective-permute-done((bf16[24,3072]{1,0:T(8,128)(2,1)S(1)}, bf16[24,3072]{1,0:T(8,128)(2,1)S(1)}, u32[]{:S(2)}, u32[]{:S(2)}) %collective-permute-start.65) | collective-permute-done | bytes 147488 | tf_op jit(solution)/shard_map/ppermute | solution.py:441
  389.3 6.5 %collective-permute-done.73 = bf16[24,3072]{1,0:T(8,128)(2,1)S(1)} collective-permute-done((bf16[24,3072]{1,0:T(8,128)(2,1)S(1)}, bf16[24,3072]{1,0:T(8,128)(2,1)S(1)}, u32[]{:S(2)}, u32[]{:S(2)}) %collective-permute-start.73) | collective-permute-done | bytes 147488 | tf_op jit(solution)/shard_map/ppermute | solution.py:441
  (339 shorter events, 87.8 us)
Async XLA Ops:
  10.5 27.8 %collective-permute-start.5 = (bf16[96,768]{1,0:T(8,128)(2,1)S(1)}, bf16[96,768]{1,0:T(8,128)(2,1)S(1)}, u32[]{:S(2)}, u32[]{:S(2)}) collective-permute-start(bf16[96,768]{1,0:T(8,128)(2,1)S(1)} %copy-done.23), channel_id=1, source_target_pairs={{0,4},{1,5},{2,6},{3,7},{4,0},{5,1},{6,2},{7,3},{8,12},{9,13},{10,... | collective-permute-start | bytes 442376 | tf_op jit(solution)/shard_map/ppermute | solution.py:441
  15.8 20.3 %collective-permute-start.2 = (bf16[96,768]{1,0:T(8,128)(2,1)S(1)}, bf16[96,768]{1,0:T(8,128)(2,1)S(1)}, u32[]{:S(2)}, u32[]{:S(2)}) collective-permute-start(bf16[96,768]{1,0:T(8,128)(2,1)S(1)} %copy-done.22), channel_id=1, source_target_pairs={{0,16},{1,17},{2,18},{3,19},{4,20},{5,21},{6,22},{7,23},{8,24},{9,... | collective-permute-start | bytes 442376 | tf_op jit(solution)/shard_map/ppermute | solution.py:441
  17.7 21.0 %collective-permute-start.14 = (bf16[96,768]{1,0:T(8,128)(2,1)S(1)}, bf16[96,768]{1,0:T(8,128)(2,1)S(1)}, u32[]{:S(2)}, u32[]{:S(2)}) collective-permute-start(bf16[96,768]{1,0:T(8,128)(2,1)S(1)} %collective-permute-done.4), channel_id=1, source_target_pairs={{0,4},{1,5},{2,6},{3,7},{4,0},{5,1},{6,2},{7,3},{8,12},{9,13},{10,... | collective-permute-start | bytes 442376 | tf_op jit(solution)/shard_map/ppermute | solution.py:441
  20.5 19.7 %collective-permute-start.13 = (bf16[48,3072]{1,0:T(8,128)(2,1)S(1)}, bf16[48,3072]{1,0:T(8,128)(2,1)S(1)}, u32[]{:S(2)}, u32[]{:S(2)}) collective-permute-start(bf16[48,3072]{1,0:T(8,128)(2,1)S(1)} %pad_maximum_fusion.5), channel_id=1, source_target_pairs={{0,24},{1,25},{2,26},{3,27},{4,28},{5,29},{6,30},{7,31},{8,0},{9,1... | collective-permute-start | bytes 884744 | tf_op jit(solution)/shard_map/ppermute | solution.py:441
  23.5 30.7 %collective-permute-start.12 = (bf16[48,3072]{1,0:T(8,128)(2,1)S(1)}, bf16[48,3072]{1,0:T(8,128)(2,1)S(1)}, u32[]{:S(2)}, u32[]{:S(2)}) collective-permute-start(bf16[48,3072]{1,0:T(8,128)(2,1)S(1)} %pad_maximum_fusion.5), channel_id=1, source_target_pairs={{0,16},{1,17},{2,18},{3,19},{4,20},{5,21},{6,22},{7,23},{8,24},{9,... | collective-permute-start | bytes 884744 | tf_op jit(solution)/shard_map/ppermute | solution.py:441
  36.1 18.1 %collective-permute-start.11 = (bf16[48,3072]{1,0:T(8,128)(2,1)S(1)}, bf16[48,3072]{1,0:T(8,128)(2,1)S(1)}, u32[]{:S(2)}, u32[]{:S(2)}) collective-permute-start(bf16[48,3072]{1,0:T(8,128)(2,1)S(1)} %pad_maximum_fusion.5), channel_id=1, source_target_pairs={{0,8},{1,9},{2,10},{3,11},{4,12},{5,13},{6,14},{7,15},{8,16},{9,17... | collective-permute-start | bytes 884744 | tf_op jit(solution)/shard_map/ppermute | solution.py:441
  38.3 16.2 %collective-permute-start.7 = (bf16[4,96,768]{2,1,0:T(8,128)(2,1)S(1)}, bf16[4,96,768]{2,1,0:T(8,128)(2,1)S(1)}, u32[]{:S(2)}, u32[]{:S(2)}) collective-permute-start(bf16[4,96,768]{2,1,0:T(8,128)(2,1)S(1)} %pad_maximum_fusion.3.refs_4_), channel_id=1, source_target_pairs={{0,4},{1,5},{2,6},{3,7},{4,0},{5,1},{6,2},{7,3},{8,12},{9,13},{10,... | collective-permute-start | bytes 1769480 | tf_op jit(solution)/shard_map/ppermute | solution.py:441
  38.7 15.8 %collective-permute-start.6 = (bf16[4,96,768]{2,1,0:T(8,128)(2,1)S(1)}, bf16[4,96,768]{2,1,0:T(8,128)(2,1)S(1)}, u32[]{:S(2)}, u32[]{:S(2)}) collective-permute-start(bf16[4,96,768]{2,1,0:T(8,128)(2,1)S(1)} %pad_maximum_fusion.3.refs_4_), channel_id=1, source_target_pairs={{0,2},{1,3},{2,0},{3,1},{4,6},{5,7},{6,4},{7,5},{8,10},{9,11},{10,... | collective-permute-start | bytes 1769480 | tf_op jit(solution)/shard_map/ppermute | solution.py:441
  54.5 24.0 %collective-permute-start.16 = (bf16[4,48,3072]{2,1,0:T(8,128)(2,1)S(1)}, bf16[4,48,3072]{2,1,0:T(8,128)(2,1)S(1)}, u32[]{:S(2)}, u32[]{:S(2)}) collective-permute-start(bf16[4,48,3072]{2,1,0:T(8,128)(2,1)S(1)} %pad_maximum_fusion.refs_6_.refs_4_.refs_25_.refs_9_), channel_id=1, source_target_pairs={{0,4},{1,5},{2,6},{3,7},{4,0},{5,1},{6,2},{7,3},{8,12},{9,13},{10,... | collective-permute-start | bytes 3538952 | tf_op jit(solution)/shard_map/ppermute | solution.py:441
  55.1 27.5 %collective-permute-start.15 = (bf16[4,48,3072]{2,1,0:T(8,128)(2,1)S(1)}, bf16[4,48,3072]{2,1,0:T(8,128)(2,1)S(1)}, u32[]{:S(2)}, u32[]{:S(2)}) collective-permute-start(bf16[4,48,3072]{2,1,0:T(8,128)(2,1)S(1)} %pad_maximum_fusion.refs_6_.refs_4_.refs_25_.refs_9_), channel_id=1, source_target_pairs={{0,2},{1,3},{2,0},{3,1},{4,6},{5,7},{6,4},{7,5},{8,10},{9,11},{10,... | collective-permute-start | bytes 3538952 | tf_op jit(solution)/shard_map/ppermute | solution.py:441
  55.6 28.1 %collective-permute-start.10 = (bf16[48,1920]{1,0:T(8,128)(2,1)S(1)}, bf16[48,1920]{1,0:T(8,128)(2,1)S(1)}, u32[]{:S(2)}, u32[]{:S(2)}) collective-permute-start(bf16[48,1920]{1,0:T(8,128)(2,1)S(1)} %get-tuple-element.47), channel_id=1, source_target_pairs={{0,24},{1,25},{2,26},{3,27},{4,28},{5,29},{6,30},{7,31},{8,0},{9,1... | collective-permute-start | bytes 552968 | tf_op jit(solution)/shard_map/ppermute | solution.py:441
  57.9 27.0 %collective-permute-start.9 = (bf16[48,1920]{1,0:T(8,128)(2,1)S(1)}, bf16[48,1920]{1,0:T(8,128)(2,1)S(1)}, u32[]{:S(2)}, u32[]{:S(2)}) collective-permute-start(bf16[48,1920]{1,0:T(8,128)(2,1)S(1)} %get-tuple-element.47), channel_id=1, source_target_pairs={{0,16},{1,17},{2,18},{3,19},{4,20},{5,21},{6,22},{7,23},{8,24},{9,... | collective-permute-start | bytes 552968 | tf_op jit(solution)/shard_map/ppermute | solution.py:441
  58.2 27.4 %collective-permute-start.8 = (bf16[48,1920]{1,0:T(8,128)(2,1)S(1)}, bf16[48,1920]{1,0:T(8,128)(2,1)S(1)}, u32[]{:S(2)}, u32[]{:S(2)}) collective-permute-start(bf16[48,1920]{1,0:T(8,128)(2,1)S(1)} %get-tuple-element.47), channel_id=1, source_target_pairs={{0,8},{1,9},{2,10},{3,11},{4,12},{5,13},{6,14},{7,15},{8,16},{9,17... | collective-permute-start | bytes 552968 | tf_op jit(solution)/shard_map/ppermute | solution.py:441
  82.6 15.1 %collective-permute-start.20 = (bf16[48,1920]{1,0:T(8,128)(2,1)S(1)}, bf16[48,1920]{1,0:T(8,128)(2,1)S(1)}, u32[]{:S(2)}, u32[]{:S(2)}) collective-permute-start(bf16[48,1920]{1,0:T(8,128)(2,1)S(1)} %get-tuple-element.50), channel_id=1, source_target_pairs={{0,16},{1,17},{2,18},{3,19},{4,20},{5,21},{6,22},{7,23},{8,24},{9,... | collective-permute-start | bytes 552968 | tf_op jit(solution)/shard_map/ppermute | solution.py:441
  87.7 24.0 %collective-permute-start.23 = (bf16[2,48,3072]{2,1,0:T(8,128)(2,1)S(1)}, bf16[2,48,3072]{2,1,0:T(8,128)(2,1)}, u32[]{:S(2)}, u32[]{:S(2)}) collective-permute-start(bf16[2,48,3072]{2,1,0:T(8,128)(2,1)S(1)} %slice.205), channel_id=1, source_target_pairs={{0,2},{1,3},{2,0},{3,1},{4,6},{5,7},{6,4},{7,5},{8,10},{9,11},{10,... | collective-permute-start | bytes 1769480 | tf_op jit(solution)/shard_map/ppermute | solution.py:441
  98.8 16.6 %collective-permute-start.24 = (bf16[4,48,3072]{2,1,0:T(8,128)(2,1)S(1)}, bf16[4,48,3072]{2,1,0:T(8,128)(2,1)}, u32[]{:S(2)}, u32[]{:S(2)}) collective-permute-start(bf16[4,48,3072]{2,1,0:T(8,128)(2,1)S(1)} %pad_maximum_fusion.refs_6_.refs_4_.refs_25_.refs_9_), channel_id=1, source_target_pairs={{0,1},{1,0},{2,3},{3,2},{4,5},{5,4},{6,7},{7,6},{8,9},{9,8},{10,11... | collective-permute-start | bytes 3538952 | tf_op jit(solution)/shard_map/ppermute | solution.py:441
  98.9 17.1 %collective-permute-start.26 = (bf16[4,48,3072]{2,1,0:T(8,128)(2,1)}, bf16[4,48,3072]{2,1,0:T(8,128)(2,1)}, u32[]{:S(2)}, u32[]{:S(2)}) collective-permute-start(bf16[4,48,3072]{2,1,0:T(8,128)(2,1)} %copy-done.12), channel_id=1, source_target_pairs={{0,1},{1,0},{2,3},{3,2},{4,5},{5,4},{6,7},{7,6},{8,9},{9,8},{10,11... | collective-permute-start | bytes 3538952 | tf_op jit(solution)/shard_map/ppermute | solution.py:441
  99.4 17.2 %collective-permute-start.25 = (bf16[4,48,3072]{2,1,0:T(8,128)(2,1)}, bf16[4,48,3072]{2,1,0:T(8,128)(2,1)}, u32[]{:S(2)}, u32[]{:S(2)}) collective-permute-start(bf16[4,48,3072]{2,1,0:T(8,128)(2,1)} %copy-done.13), channel_id=1, source_target_pairs={{0,1},{1,0},{2,3},{3,2},{4,5},{5,4},{6,7},{7,6},{8,9},{9,8},{10,11... | collective-permute-start | bytes 3538952 | tf_op jit(solution)/shard_map/ppermute | solution.py:441
  115.4 21.1 %collective-permute-start.33 = (bf16[4,96,768]{2,1,0:T(8,128)(2,1)}, bf16[4,96,768]{2,1,0:T(8,128)(2,1)}, u32[]{:S(2)}, u32[]{:S(2)}) collective-permute-start(bf16[4,96,768]{2,1,0:T(8,128)(2,1)} %pad_maximum_fusion.4.refs_5_.refs_7_), channel_id=1, source_target_pairs={{0,8},{1,9},{2,10},{3,11},{4,12},{5,13},{6,14},{7,15},{8,16},{9,17... | collective-permute-start | bytes 1769480 | tf_op jit(solution)/shard_map/ppermute | solution.py:441
  116.0 18.2 %collective-permute-start.30 = (bf16[4,48,1920]{2,1,0:T(8,128)(2,1)S(1)}, bf16[4,48,1920]{2,1,0:T(8,128)(2,1)S(1)}, u32[]{:S(2)}, u32[]{:S(2)}) collective-permute-start(bf16[4,48,1920]{2,1,0:T(8,128)(2,1)S(1)} %pad_maximum_fusion.1.refs_5_.refs_14_), channel_id=1, source_target_pairs={{0,4},{1,5},{2,6},{3,7},{4,0},{5,1},{6,2},{7,3},{8,12},{9,13},{10,... | collective-permute-start | bytes 2211848 | tf_op jit(solution)/shard_map/ppermute | solution.py:441
  116.6 17.9 %collective-permute-start.29 = (bf16[4,48,1920]{2,1,0:T(8,128)(2,1)S(1)}, bf16[4,48,1920]{2,1,0:T(8,128)(2,1)S(1)}, u32[]{:S(2)}, u32[]{:S(2)}) collective-permute-start(bf16[4,48,1920]{2,1,0:T(8,128)(2,1)S(1)} %pad_maximum_fusion.1.refs_5_.refs_14_), channel_id=1, source_target_pairs={{0,2},{1,3},{2,0},{3,1},{4,6},{5,7},{6,4},{7,5},{8,10},{9,11},{10,... | collective-permute-start | bytes 2211848 | tf_op jit(solution)/shard_map/ppermute | solution.py:441
  134.5 17.5 %collective-permute-start.32 = (bf16[4,48,1920]{2,1,0:T(8,128)(2,1)S(1)}, bf16[4,48,1920]{2,1,0:T(8,128)(2,1)}, u32[]{:S(2)}, u32[]{:S(2)}) collective-permute-start(bf16[4,48,1920]{2,1,0:T(8,128)(2,1)S(1)} %pad_maximum_fusion.2.refs_6_.refs_1_.refs_15_), channel_id=1, source_target_pairs={{0,4},{1,5},{2,6},{3,7},{4,0},{5,1},{6,2},{7,3},{8,12},{9,13},{10,... | collective-permute-start | bytes 2211848 | tf_op jit(solution)/shard_map/ppermute | solution.py:441
  136.0 16.8 %collective-permute-start.31 = (bf16[4,48,1920]{2,1,0:T(8,128)(2,1)S(1)}, bf16[4,48,1920]{2,1,0:T(8,128)(2,1)}, u32[]{:S(2)}, u32[]{:S(2)}) collective-permute-start(bf16[4,48,1920]{2,1,0:T(8,128)(2,1)S(1)} %pad_maximum_fusion.2.refs_6_.refs_1_.refs_15_), channel_id=1, source_target_pairs={{0,2},{1,3},{2,0},{3,1},{4,6},{5,7},{6,4},{7,5},{8,10},{9,11},{10,... | collective-permute-start | bytes 2211848 | tf_op jit(solution)/shard_map/ppermute | solution.py:441
  136.5 15.5 %collective-permute-start.41 = (bf16[4,96,768]{2,1,0:T(8,128)(2,1)}, bf16[4,96,768]{2,1,0:T(8,128)(2,1)}, u32[]{:S(2)}, u32[]{:S(2)}) collective-permute-start(bf16[4,96,768]{2,1,0:T(8,128)(2,1)} %collective-permute-done.33.refs_6_.refs_8_), channel_id=1, source_target_pairs={{0,8},{1,9},{2,10},{3,11},{4,12},{5,13},{6,14},{7,15},{8,16},{9,17... | collective-permute-start | bytes 1769480 | tf_op jit(solution)/shard_map/ppermute | solution.py:441
  140.0 34.7 %collective-permute-start.43 = (bf16[4,96,768]{2,1,0:T(8,128)(2,1)S(1)}, bf16[4,96,768]{2,1,0:T(8,128)(2,1)S(1)}, u32[]{:S(2)}, u32[]{:S(2)}) collective-permute-start(bf16[4,96,768]{2,1,0:T(8,128)(2,1)S(1)} %copy-done.9), channel_id=1, source_target_pairs={{0,1},{1,0},{2,3},{3,2},{4,5},{5,4},{6,7},{7,6},{8,9},{9,8},{10,11... | collective-permute-start | bytes 1769480 | tf_op jit(solution)/shard_map/ppermute | solution.py:441
  140.0 35.4 %collective-permute-start.36 = (bf16[4,48,1920]{2,1,0:T(8,128)(2,1)S(1)}, bf16[4,48,1920]{2,1,0:T(8,128)(2,1)S(1)}, u32[]{:S(2)}, u32[]{:S(2)}) collective-permute-start(bf16[4,48,1920]{2,1,0:T(8,128)(2,1)S(1)} %pad_maximum_fusion.2.refs_6_.refs_1_.refs_15_), channel_id=1, source_target_pairs={{0,1},{1,0},{2,3},{3,2},{4,5},{5,4},{6,7},{7,6},{8,9},{9,8},{10,11... | collective-permute-start | bytes 2211848 | tf_op jit(solution)/shard_map/ppermute | solution.py:441
  152.0 24.0 %collective-permute-start.44 = (bf16[4,96,768]{2,1,0:T(8,128)(2,1)}, bf16[4,96,768]{2,1,0:T(8,128)(2,1)S(1)}, u32[]{:S(2)}, u32[]{:S(2)}) collective-permute-start(bf16[4,96,768]{2,1,0:T(8,128)(2,1)} %collective-permute-done.33.refs_6_.refs_8_), channel_id=1, source_target_pairs={{0,1},{1,0},{2,3},{3,2},{4,5},{5,4},{6,7},{7,6},{8,9},{9,8},{10,11... | collective-permute-start | bytes 1769480 | tf_op jit(solution)/shard_map/ppermute | solution.py:441
  152.0 24.0 %collective-permute-start.45 = (bf16[4,96,768]{2,1,0:T(8,128)(2,1)}, bf16[4,96,768]{2,1,0:T(8,128)(2,1)S(1)}, u32[]{:S(2)}, u32[]{:S(2)}) collective-permute-start(bf16[4,96,768]{2,1,0:T(8,128)(2,1)} %collective-permute-done.41.refs_7_.refs_9_), channel_id=1, source_target_pairs={{0,1},{1,0},{2,3},{3,2},{4,5},{5,4},{6,7},{7,6},{8,9},{9,8},{10,11... | collective-permute-start | bytes 1769480 | tf_op jit(solution)/shard_map/ppermute | solution.py:441
  152.8 23.7 %collective-permute-start.42 = (bf16[4,96,768]{2,1,0:T(8,128)(2,1)}, bf16[4,96,768]{2,1,0:T(8,128)(2,1)}, u32[]{:S(2)}, u32[]{:S(2)}) collective-permute-start(bf16[4,96,768]{2,1,0:T(8,128)(2,1)} %collective-permute-done.41.refs_7_.refs_9_), channel_id=1, source_target_pairs={{0,8},{1,9},{2,10},{3,11},{4,12},{5,13},{6,14},{7,15},{8,16},{9,17... | collective-permute-start | bytes 1769480 | tf_op jit(solution)/shard_map/ppermute | solution.py:441
  176.0 15.2 %collective-permute-start.38 = (bf16[4,48,1920]{2,1,0:T(8,128)(2,1)}, bf16[4,48,1920]{2,1,0:T(8,128)(2,1)}, u32[]{:S(2)}, u32[]{:S(2)}) collective-permute-start(bf16[4,48,1920]{2,1,0:T(8,128)(2,1)} %collective-permute-done.32.refs_8_.refs_3_.refs_17_), channel_id=1, source_target_pairs={{0,1},{1,0},{2,3},{3,2},{4,5},{5,4},{6,7},{7,6},{8,9},{9,8},{10,11... | collective-permute-start | bytes 2211848 | tf_op jit(solution)/shard_map/ppermute | solution.py:441
  189.5 29.6 %collective-permute-start.49 = (bf16[4,48,1920]{2,1,0:T(8,128)(2,1)S(1)}, bf16[4,48,1920]{2,1,0:T(8,128)(2,1)}, u32[]{:S(2)}, u32[]{:S(2)}) collective-permute-start(bf16[4,48,1920]{2,1,0:T(8,128)(2,1)S(1)} %copy-done.8), channel_id=1, source_target_pairs={{0,1},{1,0},{2,3},{3,2},{4,5},{5,4},{6,7},{7,6},{8,9},{9,8},{10,11... | collective-permute-start | bytes 2211848 | tf_op jit(solution)/shard_map/ppermute | solution.py:441
  190.0 29.3 %collective-permute-start.51 = (bf16[4,48,1920]{2,1,0:T(8,128)(2,1)}, bf16[4,48,1920]{2,1,0:T(8,128)(2,1)}, u32[]{:S(2)}, u32[]{:S(2)}) collective-permute-start(bf16[4,48,1920]{2,1,0:T(8,128)(2,1)} %copy-done.14), channel_id=1, source_target_pairs={{0,1},{1,0},{2,3},{3,2},{4,5},{5,4},{6,7},{7,6},{8,9},{9,8},{10,11... | collective-permute-start | bytes 2211848 | tf_op jit(solution)/shard_map/ppermute | solution.py:441
  190.1 29.5 %collective-permute-start.50 = (bf16[4,48,1920]{2,1,0:T(8,128)(2,1)}, bf16[4,48,1920]{2,1,0:T(8,128)(2,1)}, u32[]{:S(2)}, u32[]{:S(2)}) collective-permute-start(bf16[4,48,1920]{2,1,0:T(8,128)(2,1)} %copy-done.15), channel_id=1, source_target_pairs={{0,1},{1,0},{2,3},{3,2},{4,5},{5,4},{6,7},{7,6},{8,9},{9,8},{10,11... | collective-permute-start | bytes 2211848 | tf_op jit(solution)/shard_map/ppermute | solution.py:441
  204.5 15.4 %collective-permute-start.52 = (bf16[2,48,1920]{2,1,0:T(8,128)(2,1)}, bf16[2,48,1920]{2,1,0:T(8,128)(2,1)S(1)}, u32[]{:S(2)}, u32[]{:S(2)}) collective-permute-start(bf16[2,48,1920]{2,1,0:T(8,128)(2,1)} %collective-permute-done.47.refs_8_.refs_17_), channel_id=1, source_target_pairs={{0,1},{1,0},{2,3},{3,2},{4,5},{5,4},{6,7},{7,6},{8,9},{9,8},{10,11... | collective-permute-start | bytes 1105928 | tf_op jit(solution)/shard_map/ppermute | solution.py:441
  204.5 15.6 %collective-permute-start.53 = (bf16[2,48,1920]{2,1,0:T(8,128)(2,1)}, bf16[2,48,1920]{2,1,0:T(8,128)(2,1)}, u32[]{:S(2)}, u32[]{:S(2)}) collective-permute-start(bf16[2,48,1920]{2,1,0:T(8,128)(2,1)} %collective-permute-done.48.refs_9_.refs_18_), channel_id=1, source_target_pairs={{0,1},{1,0},{2,3},{3,2},{4,5},{5,4},{6,7},{7,6},{8,9},{9,8},{10,11... | collective-permute-start | bytes 1105928 | tf_op jit(solution)/shard_map/ppermute | solution.py:441
  213.9 28.2 %all-to-all-start.1 = ((bf16[32,16,768]{2,1,0:T(8,128)(2,1)}), bf16[32,16,768]{2,1,0:T(8,128)(2,1)S(1)}, u32[]{:S(2)}, u32[]{:S(2)}) async-start(bf16[32,16,768]{2,1,0:T(8,128)(2,1)} %broadcast_in_dim.22), calls=%async_computation.1 | async-start | bytes 1572864 | tf_op jit(solution)/shard_map/all_to_all | solution.py:529
  219.1 15.4 %collective-permute-start.54 = (bf16[4,96,768]{2,1,0:T(8,128)(2,1)S(1)}, bf16[4,96,768]{2,1,0:T(8,128)(2,1)S(1)}, u32[]{:S(2)}, u32[]{:S(2)}) collective-permute-start(bf16[4,96,768]{2,1,0:T(8,128)(2,1)S(1)} %copy-done.11), channel_id=1, source_target_pairs={{0,1},{1,0},{2,3},{3,2},{4,5},{5,4},{6,7},{7,6},{8,9},{9,8},{10,11... | collective-permute-start | bytes 1769480 | tf_op jit(solution)/shard_map/ppermute | solution.py:441
  243.1 26.4 %all-to-all-start.2 = ((bf16[32,16,768]{2,1,0:T(8,128)(2,1)}), bf16[32,16,768]{2,1,0:T(8,128)(2,1)S(1)}, u32[]{:S(2)}, u32[]{:S(2)}) async-start(bf16[32,16,768]{2,1,0:T(8,128)(2,1)} %broadcast_in_dim.25), calls=%async_computation.2 | async-start | bytes 1572864 | tf_op jit(solution)/shard_map/all_to_all | solution.py:529
  308.0 24.0 %collective-permute-start.59 = (bf16[384,3072]{1,0:T(8,128)(2,1)}, bf16[384,3072]{1,0:T(8,128)(2,1)}, u32[]{:S(2)}, u32[]{:S(2)}) collective-permute-start(bf16[384,3072]{1,0:T(8,128)(2,1)} %get-tuple-element.77), channel_id=1, source_target_pairs={{0,1},{1,0},{2,3},{3,2},{4,5},{5,4},{6,7},{7,6},{8,9},{9,8},{10,11... | collective-permute-start | bytes 7077896 | tf_op jit(solution)/shard_map/ppermute | solution.py:441
  315.6 20.9 %collective-permute-start.67 = (bf16[384,3072]{1,0:T(8,128)(2,1)}, bf16[384,3072]{1,0:T(8,128)(2,1)}, u32[]{:S(2)}, u32[]{:S(2)}) collective-permute-start(bf16[384,3072]{1,0:T(8,128)(2,1)} %get-tuple-element.79), channel_id=1, source_target_pairs={{0,1},{1,0},{2,3},{3,2},{4,5},{5,4},{6,7},{7,6},{8,9},{9,8},{10,11... | collective-permute-start | bytes 7077896 | tf_op jit(solution)/shard_map/ppermute | solution.py:441
  335.1 16.2 %collective-permute-start.60 = (bf16[4,2,24,1536]{3,2,0,1:T(8,128)(2,1)S(1)}, bf16[4,2,24,1536]{3,2,0,1:T(8,128)(2,1)S(1)}, u32[]{:S(2)}, u32[]{:S(2)}) collective-permute-start(bf16[4,2,24,1536]{3,2,0,1:T(8,128)(2,1)S(1)} %fusion.7), channel_id=1, source_target_pairs={{0,2},{1,3},{2,0},{3,1},{4,6},{5,7},{6,4},{7,5},{8,10},{9,11},{10,... | collective-permute-start | bytes 1769480 | tf_op jit(solution)/shard_map/ppermute | solution.py:441
  335.7 16.4 %collective-permute-start.62 = (bf16[4,2,24,1536]{3,2,0,1:T(8,128)(2,1)S(1)}, bf16[4,2,24,1536]{3,2,0,1:T(8,128)(2,1)S(1)}, u32[]{:S(2)}, u32[]{:S(2)}) collective-permute-start(bf16[4,2,24,1536]{3,2,0,1:T(8,128)(2,1)S(1)} %fusion.8), channel_id=1, source_target_pairs={{0,4},{1,5},{2,6},{3,7},{4,0},{5,1},{6,2},{7,3},{8,12},{9,13},{10,... | collective-permute-start | bytes 1769480 | tf_op jit(solution)/shard_map/ppermute | solution.py:441
  339.7 24.3 %collective-permute-start.68 = (bf16[4,2,24,1536]{3,2,0,1:T(8,128)(2,1)S(1)}, bf16[4,2,24,1536]{3,2,0,1:T(8,128)(2,1)S(1)}, u32[]{:S(2)}, u32[]{:S(2)}) collective-permute-start(bf16[4,2,24,1536]{3,2,0,1:T(8,128)(2,1)S(1)} %fusion.9), channel_id=1, source_target_pairs={{0,2},{1,3},{2,0},{3,1},{4,6},{5,7},{6,4},{7,5},{8,10},{9,11},{10,... | collective-permute-start | bytes 1769480 | tf_op jit(solution)/shard_map/ppermute | solution.py:441
  341.1 23.7 %collective-permute-start.70 = (bf16[4,2,24,1536]{3,2,0,1:T(8,128)(2,1)S(1)}, bf16[4,2,24,1536]{3,2,0,1:T(8,128)(2,1)S(1)}, u32[]{:S(2)}, u32[]{:S(2)}) collective-permute-start(bf16[4,2,24,1536]{3,2,0,1:T(8,128)(2,1)S(1)} %fusion.10), channel_id=1, source_target_pairs={{0,4},{1,5},{2,6},{3,7},{4,0},{5,1},{6,2},{7,3},{8,12},{9,13},{10,... | collective-permute-start | bytes 1769480 | tf_op jit(solution)/shard_map/ppermute | solution.py:441
  351.5 19.4 %collective-permute-start.61 = (bf16[4,24,1536]{2,1,0:T(8,128)(2,1)S(1)}, bf16[4,24,1536]{2,1,0:T(8,128)(2,1)S(1)}, u32[]{:S(2)}, u32[]{:S(2)}) collective-permute-start(bf16[4,24,1536]{2,1,0:T(8,128)(2,1)S(1)} %fusion.15), channel_id=1, source_target_pairs={{0,4},{1,5},{2,6},{3,7},{4,0},{5,1},{6,2},{7,3},{8,12},{9,13},{10,... | collective-permute-start | bytes 884744 | tf_op jit(solution)/shard_map/ppermute | solution.py:441
  352.3 18.7 %collective-permute-start.63 = (bf16[4,24,1536]{2,1,0:T(8,128)(2,1)S(1)}, bf16[4,24,1536]{2,1,0:T(8,128)(2,1)S(1)}, u32[]{:S(2)}, u32[]{:S(2)}) collective-permute-start(bf16[4,24,1536]{2,1,0:T(8,128)(2,1)S(1)} %fusion.16), channel_id=1, source_target_pairs={{0,2},{1,3},{2,0},{3,1},{4,6},{5,7},{6,4},{7,5},{8,10},{9,11},{10,... | collective-permute-start | bytes 884744 | tf_op jit(solution)/shard_map/ppermute | solution.py:441
  377.0 18.8 %collective-permute-start.73 = (bf16[24,3072]{1,0:T(8,128)(2,1)S(1)}, bf16[24,3072]{1,0:T(8,128)(2,1)S(1)}, u32[]{:S(2)}, u32[]{:S(2)}) collective-permute-start(bf16[24,3072]{1,0:T(8,128)(2,1)S(1)} %get-tuple-element.98), channel_id=1, source_target_pairs={{0,16},{1,17},{2,18},{3,19},{4,20},{5,21},{6,22},{7,23},{8,24},{9,... | collective-permute-start | bytes 442376 | tf_op jit(solution)/shard_map/ppermute | solution.py:441
  379.9 15.9 %collective-permute-start.74 = (bf16[24,3072]{1,0:T(8,128)(2,1)S(1)}, bf16[24,3072]{1,0:T(8,128)(2,1)S(1)}, u32[]{:S(2)}, u32[]{:S(2)}) collective-permute-start(bf16[24,3072]{1,0:T(8,128)(2,1)S(1)} %get-tuple-element.99), channel_id=1, source_target_pairs={{0,24},{1,25},{2,26},{3,27},{4,28},{5,29},{6,30},{7,31},{8,0},{9,1... | collective-permute-start | bytes 442376 | tf_op jit(solution)/shard_map/ppermute | solution.py:441
  (83 other events, 923.3 us)
